TPU v7x, 32 devices: a whole 2x2x4 slice. The times are simulated.
32 devices in a mesh: group: 2 (over x), expert: 16 (over z, y, core).
Axes of the slice: x: 2, y: 2, z: 4, core: 2. Of those that a mesh axis runs over, the one named last changes fastest.
Arguments:
- tokens: bfloat16 [1536, 3584], P(('group', 'expert')), parts along dimension 0, may hold values from -6 to 6
- tangent: bfloat16 [1536, 3584], P(('group', 'expert')), parts along dimension 0, may hold values from -6 to 6
- routes: int32 [1536, 8], P(('group', 'expert')), parts along dimension 0, may hold values from 0 to 15, all different within a row; in each aligned block of 48 rows (0 to 47, 48 to 95, ...) at most 32 rows name the same one
- gates: float32 [1536, 8], P(('group', 'expert')), parts along dimension 0, may hold values from 0.1 to 1
- probes: float32 [1536, 16], P(('group', 'expert')), parts along dimension 0, may hold values from -0.21875 to 0.21875
- w_gate: bfloat16 [16, 3584, 1024], P('expert'), may hold values from -0.09375 to 0.09375
- w_up: bfloat16 [16, 3584, 1024], P('expert'), may hold values from -0.09375 to 0.09375
- w_down: bfloat16 [16, 1024, 3584], P('expert'), may hold values from -0.1875 to 0.1875
Outputs:
- curvature_rows: bfloat16 [1536, 3584], P(('group', 'expert')), parts along dimension 0
- sketch: float32 [32, 3584], P('group', 'expert'), parts along dimension 0
There are 2 independent parts, one for each index of `group`. A program takes and returns all parts, laid end to end along the dimension named above; an argument that names none is the same for every part. Nothing has to cross between parts.
Inputs may be any that keep to these rules, and one draw needn't show every extreme that they name: `routes`: within one row the 8 experts differ. In each aligned block of 48 rows (the rows of one device) no expert is named by more than 32 rows, a bound that some block reaches.
All inputs are finite; a program needn't handle non-finite values.
Results may differ from a plain program's by a relative error of at most 0.0075.
Values may be sent and summed in bfloat16 or wider, within the bound.
No kernel may reach another device: no remote copies, remote signals or barrier semaphores. Data moves between devices by JAX's collectives and lax.ppermute only.
A program may use at most 128 MiB of HBM per device.

v0:
```python
import functools

import jax
import jax.numpy as jnp
from jax import lax
from jax.experimental import pallas as pl
from jax.experimental.pallas import tpu as pltpu
from jax.sharding import PartitionSpec as P

BF16 = jnp.bfloat16
F32 = jnp.float32
PACK_BYTES = 56 * 1024 * 1024
UP_BYTES = 12 * 1024 * 1024
DOWN_BYTES = 12 * 1024 * 1024


def swap(values, perm):
    return lax.ppermute(values, "expert", perm)


def mm(left, right):
    return jnp.dot(left, right, preferred_element_type=F32)


def mm_t(left, right):
    return lax.dot_general(left, right, (((1,), (1,)), ((), ())), preferred_element_type=F32)


def tile_of(size, most):
    for tile in range(min(size, most), 0, -128):
        if size % tile == 0 and tile % 128 == 0:
            return tile
    return size


def load_all(copies):
    for copy in copies:
        copy.start()
    for copy in copies:
        copy.wait()


def pack_kernel(count, tokens, tangent, routes_in, gates_in, probes_in, out, whole, routes, gates, probes, sems):
    rows, width = tokens.shape
    lanes = whole.shape[1] - width
    large = [
        pltpu.make_async_copy(source, whole.at[pl.ds(j * rows, rows), pl.ds(0, width)], sems.at[j])
        for j, source in enumerate((tokens, tangent))
    ]
    small = ((routes_in, routes), (gates_in, gates), (probes_in, probes))
    early = [pltpu.make_async_copy(*both, sems.at[2 + j]) for j, both in enumerate(small)]
    for copy in early + large:
        copy.start()
    for copy in early:
        copy.wait()

    def split_up(values):
        parts = []
        for _ in range(3):
            parts.append(values.astype(BF16).astype(F32))
            values = values - parts[-1]
        parts.append(jnp.zeros((lanes - 3 * values.shape[0], rows), F32))
        return jnp.concatenate(parts, axis=0).T.astype(BF16)

    expert = lax.broadcasted_iota(jnp.int32, (count, rows), 0)
    dense = jnp.zeros((count, rows), F32)
    for k in range(routes.shape[0]):
        dense = dense + jnp.where(routes[k : k + 1, :] == expert, gates[k : k + 1, :], 0.0)
    whole[pl.ds(0, rows), pl.ds(width, lanes)] = split_up(dense)
    whole[pl.ds(rows, rows), pl.ds(width, lanes)] = split_up(probes[...])
    for copy in large:
        copy.wait()
    last = pltpu.make_async_copy(whole, out, sems.at[5])
    last.start()
    last.wait()


def pack_call(tokens, tangent, routes, gates, probes, count, lanes):
    rows, width = tokens.shape
    return pl.pallas_call(
        functools.partial(pack_kernel, count),
        in_specs=[ANY] * 5,
        out_specs=ANY,
        out_shape=jax.ShapeDtypeStruct((2 * rows, width + lanes), BF16),
        scratch_shapes=[pltpu.VMEM((2 * rows, width + lanes), BF16)]
        + [pltpu.VMEM(small.shape[::-1], small.dtype) for small in (routes, gates, probes)]
        + [pltpu.SemaphoreType.DMA((6,))],
        compiler_params=pltpu.CompilerParams(vmem_limit_bytes=PACK_BYTES),
    )(tokens, tangent, routes.T, gates.T, probes.T)


def up_kernel(f_tile, d_tile, count, *refs):
    pieces, refs = refs[:4], refs[4:]
    me, w_g, w_u, w_d, keep, send, u_out, v_out, probes_out, x_all, gates, probes, th_all, sems = refs
    width, hidden = w_g.shape
    rows = pieces[0].shape[0] // 2
    block = 4 * rows
    half = block // 2
    copies = []
    for j, piece in enumerate(pieces):
        for part in range(2):
            source = piece.at[pl.ds(part * rows, rows), pl.ds(0, width)]
            target = x_all.at[pl.ds(part * block + j * rows, rows)]
            copies.append(pltpu.make_async_copy(source, target, sems.at[4 * j + part]))
            source = piece.at[pl.ds(part * rows, rows), pl.ds(width, gates.shape[1])]
            target = (gates, probes)[part].at[pl.ds(j * rows, rows)]
            copies.append(pltpu.make_async_copy(source, target, sems.at[4 * j + 2 + part]))
    load_all(copies)
    lane = lax.broadcasted_iota(jnp.int32, gates.shape, 1) - me[0]
    hit = (lane == 0) | (lane == count) | (lane == 2 * count)
    g = jnp.sum(jnp.where(hit, gates[...].astype(F32), 0.0), axis=1, keepdims=True)
    probes_out[...] = probes[...].astype(F32).T.astype(BF16)

    def first(i, carry):
        cols = pl.ds(pl.multiple_of(i * f_tile, f_tile), f_tile)
        x = x_all[...]
        both_a = mm(x, w_g[:, cols])
        both_b = mm(x, w_u[:, cols])
        a, ta = both_a[:block], both_a[block:]
        b, tb = both_b[:block], both_b[block:]
        sig = jax.nn.sigmoid(a)
        u = (sig * (1.0 + a * (1.0 - sig))) * b * g
        v = a * sig * g
        u_out[:, cols] = u
        v_out[:, cols] = v
        th_all[:, cols] = (u * ta + v * tb).astype(BF16)
        return carry

    lax.fori_loop(0, hidden // f_tile, first, 0)

    def second(i, carry):
        cols = pl.ds(pl.multiple_of(i * d_tile, d_tile), d_tile)
        out = mm(th_all[...], w_d[:, cols]).astype(BF16)
        keep[:, cols] = out[:half]
        send[:, cols] = out[half:]
        return carry

    lax.fori_loop(0, width // d_tile, second, 0)


def down_kernel(f_tile, d_tile, rank, *refs):
    pieces, refs = refs[:4], refs[4:]
    u_in, v_in, probes, before, w_g, w_u, w_d, keep, send, term, x_all, ga, gb, sems = refs
    half = u_in.shape[0] // 2
    width, hidden = w_g.shape
    rows = pieces[0].shape[0]
    load_all(
        [
            pltpu.make_async_copy(piece, x_all.at[pl.ds(j * rows, rows)], sems.at[j])
            for j, piece in enumerate(pieces)
        ]
    )

    def first(i, carry):
        cols = pl.ds(pl.multiple_of(i * f_tile, f_tile), f_tile)
        gh = mm_t(x_all[...], w_d[cols, :])
        ga[:, cols] = (gh * u_in[:, cols]).astype(BF16)
        gb[:, cols] = (gh * v_in[:, cols]).astype(BF16)
        return carry

    lax.fori_loop(0, hidden // f_tile, first, 0)

    def second(i, carry):
        cols = pl.ds(pl.multiple_of(i * d_tile, d_tile), d_tile)
        out = (mm_t(ga[...], w_g[cols, :]) + mm_t(gb[...], w_u[cols, :])).astype(BF16)
        keep[:, cols] = out[:half]
        send[:, cols] = out[half:]
        parts = mm(probes[...], out)
        term[:, cols] = before[:, cols] + (parts[:rank] + parts[rank : 2 * rank] + parts[2 * rank : 3 * rank])
        return carry

    lax.fori_loop(0, width // d_tile, second, 0)


ANY = pl.BlockSpec(memory_space=pl.ANY)
WHOLE = pl.BlockSpec(memory_space=pltpu.VMEM)


def up_call(pieces, me, count, w_g, w_u, w_d):
    width, hidden = w_g.shape
    block, lanes = 2 * pieces[0].shape[0], pieces[0].shape[1] - width
    return pl.pallas_call(
        functools.partial(up_kernel, tile_of(hidden, 512), tile_of(width, 1792), count),
        in_specs=[ANY] * 4 + [pl.BlockSpec(memory_space=pltpu.SMEM)] + [WHOLE] * 3,
        out_specs=[WHOLE] * 5,
        out_shape=[jax.ShapeDtypeStruct((block // 2, width), BF16)] * 2
        + [jax.ShapeDtypeStruct((block, hidden), F32)] * 2
        + [jax.ShapeDtypeStruct((lanes, block), BF16)],
        scratch_shapes=[
            pltpu.VMEM((2 * block, width), BF16),
            pltpu.VMEM((block, lanes), BF16),
            pltpu.VMEM((block, lanes), BF16),
            pltpu.VMEM((block, hidden), BF16),
            pltpu.SemaphoreType.DMA((16,)),
        ],
        compiler_params=pltpu.CompilerParams(vmem_limit_bytes=UP_BYTES),
        cost_estimate=pl.CostEstimate(flops=10 * width * hidden * block, bytes_accessed=2**20, transcendentals=0),
    )(*pieces, me, w_g, w_u, w_d)


def down_call(pieces, u, v, probes, before, w_g, w_u, w_d):
    width, hidden = w_g.shape
    rank = before.shape[0]
    block = u.shape[0]
    return pl.pallas_call(
        functools.partial(down_kernel, tile_of(hidden, 512), tile_of(width, 1792), rank),
        in_specs=[ANY] * 4 + [WHOLE] * 7,
        out_specs=[WHOLE] * 3,
        out_shape=[jax.ShapeDtypeStruct((block // 2, width), BF16)] * 2 + [jax.ShapeDtypeStruct((rank, width), F32)],
        scratch_shapes=[
            pltpu.VMEM((block, width), BF16),
            pltpu.VMEM((block, hidden), BF16),
            pltpu.VMEM((block, hidden), BF16),
            pltpu.SemaphoreType.DMA((4,)),
        ],
        compiler_params=pltpu.CompilerParams(vmem_limit_bytes=DOWN_BYTES),
        cost_estimate=pl.CostEstimate(flops=6 * width * hidden * block, bytes_accessed=2**20, transcendentals=0),
    )(*pieces, u, v, probes, before, w_g, w_u, w_d)


def arrange_kernel(me, term, out):
    depth, share = out.shape[1], out.shape[3]
    plane, spot = me[0] // 4, me[0] % 4
    for d in range(4 * depth):
        back = lax.rem(plane + (depth - d // 4), depth)
        gap = spot ^ (d % 4)
        piece = (gap >> 1) | ((gap & 1) << 1)
        out[piece, back] = term[:, d * share : (d + 1) * share]


def arrange_call(term, me, count):
    rank, width = term.shape
    return pl.pallas_call(
        arrange_kernel,
        in_specs=[pl.BlockSpec(memory_space=pltpu.SMEM), WHOLE],
        out_specs=WHOLE,
        out_shape=jax.ShapeDtypeStruct((4, count // 4, rank, width // count), F32),
        compiler_params=pltpu.CompilerParams(vmem_limit_bytes=4 * 1024 * 1024),
    )(me, term)


def phase(own, split, lead, compute, turns, side, ring, across, pair, depth):
    near, far, near_mate = [own], [], []
    pieces, made, extras, ready = {}, {}, {}, {}
    moving = None
    for turn in range(2 * depth - lead):
        flight = {}
        if turn < depth:
            if turn < depth - 1:
                flight["near"] = swap(near[turn], ring)
                flight["far"] = swap(near[turn], across)
            elif split is None:
                flight["far"] = swap(near[turn], across)
            else:
                flight["far_low"] = swap(near[turn][:split], across)
                flight["far_high"] = swap(far[turn - 1][split:], ring)
            flight["near_mate"] = swap(near[turn], pair)
        if 0 <= turn - 1 < depth:
            back = turn - 1
            pieces[back] = (near[back], far[back], near_mate[back], swap(far[back], pair))
        if turn in turns:
            flight["made"] = compute(turns[turn], pieces.pop(turns[turn]))
        flight["pieces"] = dict(pieces)
        if turn - 1 in turns:
            keep, send = made[turns[turn - 1]]
            rows = keep.shape[0] // 2
            got = swap(send, pair)
            base = (keep[:rows].astype(F32) + got[:rows].astype(F32)).astype(BF16)
            outward = (keep[rows:].astype(F32) + got[rows:].astype(F32)).astype(BF16)
            flight["ready"] = (base, outward)
        due = turn - depth + 1 + lead
        if due >= 1:
            if due % depth in ready:
                due_base, crossing = ready.pop(due % depth)
            else:
                due_base, crossing = flight.pop("ready")
                flight["base"] = due_base
            flight["cross"] = swap(crossing, across)
            if due > 1:
                flight["moving"] = swap(moving, ring)
        if side is not None:
            flight["side"] = side[0](turn, extras)
        flight["waiting"] = dict(ready)
        names = list(flight)
        flight = dict(zip(names, lax.optimization_barrier([flight[name] for name in names])))
        if "near" in flight:
            near.append(flight["near"])
        if "far" in flight:
            far.append(flight["far"])
        if "far_low" in flight:
            far.append(jnp.concatenate([flight["far_low"], flight["far_high"]], axis=0))
        if "near_mate" in flight:
            near_mate.append(flight["near_mate"])
        pieces = flight["pieces"]
        if "made" in flight:
            made[turns[turn]] = flight["made"][:2]
            extras[turns[turn]] = flight["made"][2]
            if side is not None:
                side[1](turn, flight["made"][2])
        elif side is not None and turn > depth:
            side[1](turn, flight["side"])
        ready = flight["waiting"]
        if "ready" in flight:
            ready[turns[turn - 1]] = flight["ready"]
        if due >= 1:
            due_base = flight.get("base", due_base)
            total = due_base.astype(F32) + flight["cross"].astype(F32)
            if "moving" in flight:
                total = total + flight["moving"].astype(F32)
            moving = total.astype(BF16)
    return moving, extras, flight.get("side")


def body(tokens, tangent, routes, gates, probes, w_gate, w_up, w_down):
    rows, width = tokens.shape
    count = lax.axis_size("expert")
    depth = count // 4
    ring = [(i, (i + 4) % count) for i in range(count)]
    across = [(i, i ^ 2) for i in range(count)]
    pair = [(i, i ^ 1) for i in range(count)]
    w_g, w_u, w_d = w_gate[0], w_up[0], w_down[0]
    me = lax.axis_index("expert")

    rank = probes.shape[1]
    lanes = -(-3 * max(count, rank) // 128) * 128
    stacked = pack_call(tokens, tangent, routes, gates, probes, count, lanes)
    mine = jnp.full((1,), me, jnp.int32)
    weights = (w_g, w_u, w_d)

    def up(s, pieces):
        keep, send, u, v, spread = up_call(pieces, mine, count, *weights)
        return keep, send, (u, v, spread)

    turns = {s + 1: s for s in range(depth)}
    combined, saved, _ = phase(stacked, rows * 2 // 3, 1, up, turns, None, ring, across, pair, depth)

    share = width // count
    held = {"sum": jnp.zeros((rank, width), F32)}

    def down(s, pieces):
        keep, send, term = down_call(pieces, *saved[s], held["sum"], *weights)
        return keep, send, term

    def side(turn, terms):
        if turn == depth + 1:
            term = arrange_call(held["sum"], mine, count)
            held["sum"] = term[:2] + swap(term[2:], pair)
        elif turn == depth + 2:
            held["sum"] = held["sum"][0] + swap(held["sum"][1], across)
        elif turn == depth + 3:
            term = held["sum"]
            total = term[0]
            for s in range(1, depth):
                back = [(i, (i - 4 * s) % count) for i in range(count)]
                total = total + swap(term[s], back)
            held["sum"] = total
        elif turn <= depth:
            return ()
        return held["sum"]

    def settle(turn, values):
        held["sum"] = values

    turns = {s + 1: s for s in range(depth)}
    curvature_rows, _, sketch = phase(combined, None, 0, down, turns, (side, settle), ring, across, pair, depth)
    return (curvature_rows, sketch)


def solution(mesh):
    return jax.shard_map(
        body,
        mesh=mesh,
        in_specs=(
            P(("group", "expert"), None),
            P(("group", "expert"), None),
            P(("group", "expert"), None),
            P(("group", "expert"), None),
            P(("group", "expert"), None),
            P("expert", None, None),
            P("expert", None, None),
            P("expert", None, None),
        ),
        out_specs=(P(("group", "expert"), None), P("group", "expert")),
        check_vma=False,
    )
```

profile of v0, /device:TPU:0, one launch (start us, length us, event | category | flops | bytes accessed | tf_op | source)
XLA Modules:
  0.0 218.8 jit_solution(9119740027867397370)
XLA Ops:
  0.6 2.0 shard_map.95.refs_0_
  2.7 3.1 %collective-permute-start = (bf16[96,3712]{1,0:T(8,128)(2,1)}, bf16[96,3712]{1,0:T(8,128)(2,1)S(1)}, u32[]{:S(2)}, u32[]{:S(2)}) collective-permute-start(bf16[96,3712]{1,0:T(8,128)(2,1)} %shard_map.95.refs_0_), channel_id=1, source_target_pairs={{0,4},{1,5},{2,6},{3,7},{4,8},{5,9},{6,10},{7,11},{8,12},{9,13},{1... | collective-permute-start | bytes 2138120 | tf_op jit(solution)/shard_map/ppermute | solution.py:18
  5.8 1.5 collective-permute-start.1
  7.3 16.7 %collective-permute-done.refs_0_ = bf16[96,3712]{1,0:T(8,128)(2,1)S(1)} collective-permute-done((bf16[96,3712]{1,0:T(8,128)(2,1)}, bf16[96,3712]{1,0:T(8,128)(2,1)S(1)}, u32[]{:S(2)}, u32[]{:S(2)}) %collective-permute-start) | collective-permute-done | bytes 712736 | tf_op jit(solution)/shard_map/ppermute | solution.py:18
  24.0 0.9 copy-done.7
  24.8 1.1 collective-permute-start.3
  25.9 1.5 collective-permute-start.4
  27.5 3.1 %copy-done = bf16[1,3584,1024]{2,1,0:T(8,128)(2,1)S(1)} copy-done((bf16[1,3584,1024]{2,1,0:T(8,128)(2,1)S(1)}, bf16[1,3584,1024]{2,1,0:T(8,128)(2,1)}, u32[]{:S(2)}) %copy-start) | copy-done | bytes 7340056
  30.6 3.1 %copy-done.2 = bf16[1,3584,1024]{2,1,0:T(8,128)(2,1)S(1)} copy-done((bf16[1,3584,1024]{2,1,0:T(8,128)(2,1)S(1)}, bf16[1,3584,1024]{2,1,0:T(8,128)(2,1)}, u32[]{:S(2)}) %copy-start.2) | copy-done | bytes 7340056
  33.6 3.1 %copy-done.3 = bf16[1,1024,3584]{2,1,0:T(8,128)(2,1)S(1)} copy-done((bf16[1,1024,3584]{2,1,0:T(8,128)(2,1)S(1)}, bf16[1,1024,3584]{2,1,0:T(8,128)(2,1)}, u32[]{:S(2)}) %copy-start.3) | copy-done | bytes 7340056
  36.7 1.1 copy-done.4
  37.8 1.1 copy-done.8
  38.9 10.0 %shard_map.96 = (bf16[96,3584]{1,0:T(8,128)(2,1)S(1)}, bf16[96,3584]{1,0:T(8,128)(2,1)S(1)}, f32[192,1024]{1,0:T(8,128)S(1)}, f32[192,1024]{1,0:T(8,128)S(1)}, bf16[128,192]{1,0:T(8,128)(2,1)S(1)}) custom-call(bf16[96,3712]{1,0:T(8,128)(2,1)S(1)} %copy-done.4, bf16[96,3712]{1,0:T(8,128)(2,1)} %collective-permute-done.1.refs_1_, ...), custom_call_target="tpu_custom_call" | custom-call | flops 7046430720 | bytes 1048576 | tf_op jit(solution)/shard_map/pallas_call | solution.py:182
  49.0 0.9 copy-done.5
  50.3 1.6 collective-permute-start.7
  53.0 0.9 add_convert_fusion.22
  53.9 1.8 collective-permute-done.10.refs_3_
  55.7 1.9 copy-done.6
  57.6 8.7 %shard_map.97 = (bf16[96,3584]{1,0:T(8,128)(2,1)S(1)}, bf16[96,3584]{1,0:T(8,128)(2,1)S(1)}, f32[192,1024]{1,0:T(8,128)S(1)}, f32[192,1024]{1,0:T(8,128)S(1)}, bf16[128,192]{1,0:T(8,128)(2,1)S(1)}) custom-call(bf16[96,3712]{1,0:T(8,128)(2,1)S(1)} %collective-permute-done.refs_0_, bf16[96,3712]{1,0:T(8,128)(2,1)S(1)} %collective-permute-done.4.refs_1_, ...), custom_call_target="tpu_custom_call" | custom-call | flops 7046430720 | bytes 1048576 | tf_op jit(solution)/shard_map/pallas_call | solution.py:182
  66.3 3.7 %collective-permute-done.7.refs_0_ = bf16[96,3712]{1,0:T(8,128)(2,1)S(1)} collective-permute-done((bf16[96,3712]{1,0:T(8,128)(2,1)S(1)}, bf16[96,3712]{1,0:T(8,128)(2,1)S(1)}, u32[]{:S(2)}, u32[]{:S(2)}) %collective-permute-start.7) | collective-permute-done | bytes 712736 | tf_op jit(solution)/shard_map/ppermute | solution.py:18
  71.2 1.5 collective-permute-start.12
  72.9 0.9 collective-permute-start.17
  73.8 8.7 %shard_map.98 = (bf16[96,3584]{1,0:T(8,128)(2,1)S(1)}, bf16[96,3584]{1,0:T(8,128)(2,1)S(1)}, f32[192,1024]{1,0:T(8,128)S(1)}, f32[192,1024]{1,0:T(8,128)S(1)}, bf16[128,192]{1,0:T(8,128)(2,1)S(1)}) custom-call(bf16[96,3712]{1,0:T(8,128)(2,1)S(1)} %collective-permute-done.3.refs_0_, bf16[96,3712]{1,0:T(8,128)(2,1)S(1)} %collective-permute-done.8.refs_1_, ...), custom_call_target="tpu_custom_call" | custom-call | flops 7046430720 | bytes 1048576 | tf_op jit(solution)/shard_map/pallas_call | solution.py:182
  82.5 3.2 %collective-permute-done.13 = bf16[64,3712]{1,0:T(8,128)(2,1)S(1)} collective-permute-done((bf16[64,3712]{1,0:T(8,128)(2,1)S(1)}, bf16[64,3712]{1,0:T(8,128)(2,1)S(1)}, u32[]{:S(2)}, u32[]{:S(2)}) %collective-permute-start.13) | collective-permute-done | bytes 475168 | tf_op jit(solution)/shard_map/ppermute | solution.py:18
  85.8 0.7 collective-permute-done.17
  86.5 1.5 collective-permute-start.21
  88.7 1.5 collective-permute-done.19
  90.4 0.7 collective-permute-start.20
  91.2 8.7 %shard_map.99 = (bf16[96,3584]{1,0:T(8,128)(2,1)S(1)}, bf16[96,3584]{1,0:T(8,128)(2,1)S(1)}, f32[192,1024]{1,0:T(8,128)S(1)}, f32[192,1024]{1,0:T(8,128)S(1)}, bf16[128,192]{1,0:T(8,128)(2,1)S(1)}) custom-call(bf16[96,3712]{1,0:T(8,128)(2,1)S(1)} %collective-permute-done.7.refs_0_, bf16[96,3712]{1,0:T(8,128)(2,1)S(1)} %constant_dynamic-update-slice_fusion.refs_1_, ...), custom_call_target="tpu_custom_call" | custom-call | flops 7046430720 | bytes 1048576 | tf_op jit(solution)/shard_map/pallas_call | solution.py:182
  99.9 0.6 collective-permute-done.20
  100.7 1.2 collective-permute-start.24
  101.9 0.8 collective-permute-done.22
  102.8 0.8 collective-permute-start.23
  103.6 9.4 %collective-permute-done.24 = bf16[48,3584]{1,0:T(8,128)(2,1)S(1)} collective-permute-done((bf16[48,3584]{1,0:T(8,128)(2,1)S(1)}, bf16[48,3584]{1,0:T(8,128)(2,1)S(1)}, u32[]{:S(2)}, u32[]{:S(2)}) %collective-permute-start.24) | collective-permute-done | bytes 344096 | tf_op jit(solution)/shard_map/ppermute | solution.py:18
  113.1 1.4 collective-permute-start.26
  114.6 1.3 collective-permute-start.25
  115.9 8.8 %collective-permute-done.26 = bf16[48,3584]{1,0:T(8,128)(2,1)S(1)} collective-permute-done((bf16[48,3584]{1,0:T(8,128)(2,1)S(1)}, bf16[48,3584]{1,0:T(8,128)(2,1)S(1)}, u32[]{:S(2)}, u32[]{:S(2)}) %collective-permute-start.26) | collective-permute-done | bytes 344096 | tf_op jit(solution)/shard_map/ppermute | solution.py:18
  124.8 0.8 collective-permute-start.27
  125.6 1.3 collective-permute-start.28
  127.0 8.5 %collective-permute-done.27.refs_0_ = bf16[48,3584]{1,0:T(8,128)(2,1)S(1)} collective-permute-done((bf16[48,3584]{1,0:T(8,128)(2,1)S(1)}, bf16[48,3584]{1,0:T(8,128)(2,1)S(1)}, u32[]{:S(2)}, u32[]{:S(2)}) %collective-permute-start.27) | collective-permute-done | bytes 344096 | tf_op jit(solution)/shard_map/ppermute | solution.py:18
  135.5 0.8 collective-permute-start.31
  136.4 0.7 collective-permute-done.33.refs_3_
  137.1 8.8 %shard_map.100 = (bf16[96,3584]{1,0:T(8,128)(2,1)S(1)}, bf16[96,3584]{1,0:T(8,128)(2,1)S(1)}, f32[16,3584]{1,0:T(8,128)S(1)}) custom-call(bf16[48,3584]{1,0:T(8,128)(2,1)S(1)} %add_convert_fusion.12.refs_0_, bf16[48,3584]{1,0:T(8,128)(2,1)S(1)} %collective-permute-done.28.refs_1_, bf16[48,3584]{1,0:T(8,128)(2,1)S(1)} %collective-permute-done.29.refs_2_, ...), custom_call_target="tpu_custom_call" | custom-call | flops 4227858432 | bytes 1048576 | tf_op jit(solution)/shard_map/pallas_call | solution.py:205
  146.0 1.7 collective-permute-done.30.refs_0_
  148.3 0.7 collective-permute-start.35
  149.4 8.8 %shard_map.101 = (bf16[96,3584]{1,0:T(8,128)(2,1)S(1)}, bf16[96,3584]{1,0:T(8,128)(2,1)S(1)}, f32[16,3584]{1,0:T(8,128)S(1)}) custom-call(bf16[48,3584]{1,0:T(8,128)(2,1)S(1)} %collective-permute-done.27.refs_0_, bf16[48,3584]{1,0:T(8,128)(2,1)S(1)} %collective-permute-done.31.refs_1_, bf16[48,3584]{1,0:T(8,128)(2,1)S(1)} %collective-permute-done.32.refs_2_, ...), custom_call_target="tpu_custom_call" | custom-call | flops 4227858432 | bytes 1048576 | tf_op jit(solution)/shard_map/pallas_call | solution.py:205
  158.4 1.7 collective-permute-done.34.refs_0_
  160.6 0.7 collective-permute-start.39
  161.7 8.8 %shard_map.102 = (bf16[96,3584]{1,0:T(8,128)(2,1)S(1)}, bf16[96,3584]{1,0:T(8,128)(2,1)S(1)}, f32[16,3584]{1,0:T(8,128)S(1)}) custom-call(bf16[48,3584]{1,0:T(8,128)(2,1)S(1)} %collective-permute-done.30.refs_0_, bf16[48,3584]{1,0:T(8,128)(2,1)S(1)} %collective-permute-done.35.refs_1_, bf16[48,3584]{1,0:T(8,128)(2,1)S(1)} %collective-permute-done.36.refs_2_, ...), custom_call_target="tpu_custom_call" | custom-call | flops 4227858432 | bytes 1048576 | tf_op jit(solution)/shard_map/pallas_call | solution.py:205
  171.4 1.0 collective-permute-start.45
  172.5 8.8 %shard_map.103 = (bf16[96,3584]{1,0:T(8,128)(2,1)S(1)}, bf16[96,3584]{1,0:T(8,128)(2,1)S(1)}, f32[16,3584]{1,0:T(8,128)S(1)}) custom-call(bf16[48,3584]{1,0:T(8,128)(2,1)S(1)} %collective-permute-done.34.refs_0_, bf16[48,3584]{1,0:T(8,128)(2,1)S(1)} %collective-permute-done.39.refs_1_, bf16[48,3584]{1,0:T(8,128)(2,1)S(1)} %collective-permute-done.40.refs_2_, ...), custom_call_target="tpu_custom_call" | custom-call | flops 4227858432 | bytes 1048576 | tf_op jit(solution)/shard_map/pallas_call | solution.py:205
  182.4 1.3 collective-permute-start.47
  184.3 10.1 %collective-permute-done.48 = bf16[48,3584]{1,0:T(8,128)(2,1)S(1)} collective-permute-done((bf16[48,3584]{1,0:T(8,128)(2,1)S(1)}, bf16[48,3584]{1,0:T(8,128)(2,1)S(1)}, u32[]{:S(2)}, u32[]{:S(2)}) %collective-permute-start.48) | collective-permute-done | bytes 344096 | tf_op jit(solution)/shard_map/ppermute | solution.py:18
  194.5 1.3 collective-permute-start.50
  195.8 0.8 collective-permute-start.52
  196.6 8.6 %collective-permute-done.52 = f32[4,16,224]{2,1,0:T(8,128)S(1)} collective-permute-done((f32[4,16,224]{2,1,0:T(8,128)S(1)}, f32[4,16,224]{2,1,0:T(8,128)S(1)}, u32[]{:S(2)}, u32[]{:S(2)}) %collective-permute-start.52) | collective-permute-done | bytes 57376 | tf_op jit(solution)/shard_map/ppermute | solution.py:18
  205.7 0.7 collective-permute-start.54
  206.4 1.1 collective-permute-start.53
  207.4 3.5 %collective-permute-start.55 = (f32[16,224]{1,0:T(8,128)S(1)}, f32[16,224]{1,0:T(8,128)S(1)}, u32[]{:S(2)}, u32[]{:S(2)}) collective-permute-start(f32[16,224]{1,0:T(8,128)S(1)} %get-tuple-element.280), channel_id=1, source_target_pairs={{0,12},{1,13},{2,14},{3,15},{4,0},{5,1},{6,2},{7,3},{8,4},{9,5},{1... | collective-permute-start | bytes 43016 | tf_op jit(solution)/shard_map/ppermute | solution.py:18
  210.9 1.9 collective-permute-start.57
  212.9 0.9 collective-permute-done.55
  213.8 3.5 %collective-permute-done.56 = f32[16,224]{1,0:T(8,128)S(1)} collective-permute-done((f32[16,224]{1,0:T(8,128)S(1)}, f32[16,224]{1,0:T(8,128)S(1)}, u32[]{:S(2)}, u32[]{:S(2)}) %collective-permute-start.56) | collective-permute-done | bytes 14368 | tf_op jit(solution)/shard_map/ppermute | solution.py:18
  217.3 0.6 fusion.1
  217.9 0.9 add_convert_fusion
  (119 shorter events, 10.1 us)
Async XLA Ops:
  2.7 21.3 %collective-permute-start = (bf16[96,3712]{1,0:T(8,128)(2,1)}, bf16[96,3712]{1,0:T(8,128)(2,1)S(1)}, u32[]{:S(2)}, u32[]{:S(2)}) collective-permute-start(bf16[96,3712]{1,0:T(8,128)(2,1)} %shard_map.95.refs_0_), channel_id=1, source_target_pairs={{0,4},{1,5},{2,6},{3,7},{4,8},{5,9},{6,10},{7,11},{8,12},{9,13},{1... | collective-permute-start | bytes 2138120 | tf_op jit(solution)/shard_map/ppermute | solution.py:18
  5.8 18.2 %collective-permute-start.1 = (bf16[96,3712]{1,0:T(8,128)(2,1)}, bf16[96,3712]{1,0:T(8,128)(2,1)}, u32[]{:S(2)}, u32[]{:S(2)}) collective-permute-start(bf16[96,3712]{1,0:T(8,128)(2,1)} %shard_map.95.refs_0_), channel_id=1, source_target_pairs={{0,2},{1,3},{2,0},{3,1},{4,6},{5,7},{6,4},{7,5},{8,10},{9,11},{10,... | collective-permute-start | bytes 2138120 | tf_op jit(solution)/shard_map/ppermute | solution.py:18
  7.3 16.7 %collective-permute-start.2 = (bf16[96,3712]{1,0:T(8,128)(2,1)}, bf16[96,3712]{1,0:T(8,128)(2,1)S(1)}, u32[]{:S(2)}, u32[]{:S(2)}) collective-permute-start(bf16[96,3712]{1,0:T(8,128)(2,1)} %shard_map.95.refs_0_), channel_id=1, source_target_pairs={{0,1},{1,0},{2,3},{3,2},{4,5},{5,4},{6,7},{7,6},{8,9},{9,8},{10,11... | collective-permute-start | bytes 2138120 | tf_op jit(solution)/shard_map/ppermute | solution.py:18
  24.8 2.6 %collective-permute-start.6 = (bf16[96,3712]{1,0:T(8,128)(2,1)}, bf16[96,3712]{1,0:T(8,128)(2,1)}, u32[]{:S(2)}, u32[]{:S(2)}) collective-permute-start(bf16[96,3712]{1,0:T(8,128)(2,1)} %collective-permute-done.1.refs_1_), channel_id=1, source_target_pairs={{0,1},{1,0},{2,3},{3,2},{4,5},{5,4},{6,7},{7,6},{8,9},{9,8},{10,11... | collective-permute-start | bytes 2138120 | tf_op jit(solution)/shard_map/ppermute | solution.py:18
  24.8 24.1 %collective-permute-start.3 = (bf16[96,3712]{1,0:T(8,128)(2,1)S(1)}, bf16[96,3712]{1,0:T(8,128)(2,1)S(1)}, u32[]{:S(2)}, u32[]{:S(2)}) collective-permute-start(bf16[96,3712]{1,0:T(8,128)(2,1)S(1)} %collective-permute-done.refs_0_), channel_id=1, source_target_pairs={{0,4},{1,5},{2,6},{3,7},{4,8},{5,9},{6,10},{7,11},{8,12},{9,13},{1... | collective-permute-start | bytes 2138120 | tf_op jit(solution)/shard_map/ppermute | solution.py:18
  25.9 23.0 %collective-permute-start.4 = (bf16[96,3712]{1,0:T(8,128)(2,1)S(1)}, bf16[96,3712]{1,0:T(8,128)(2,1)S(1)}, u32[]{:S(2)}, u32[]{:S(2)}) collective-permute-start(bf16[96,3712]{1,0:T(8,128)(2,1)S(1)} %collective-permute-done.refs_0_), channel_id=1, source_target_pairs={{0,2},{1,3},{2,0},{3,1},{4,6},{5,7},{6,4},{7,5},{8,10},{9,11},{10,... | collective-permute-start | bytes 2138120 | tf_op jit(solution)/shard_map/ppermute | solution.py:18
  27.5 21.5 %collective-permute-start.5 = (bf16[96,3712]{1,0:T(8,128)(2,1)S(1)}, bf16[96,3712]{1,0:T(8,128)(2,1)S(1)}, u32[]{:S(2)}, u32[]{:S(2)}) collective-permute-start(bf16[96,3712]{1,0:T(8,128)(2,1)S(1)} %collective-permute-done.refs_0_), channel_id=1, source_target_pairs={{0,1},{1,0},{2,3},{3,2},{4,5},{5,4},{6,7},{7,6},{8,9},{9,8},{10,11... | collective-permute-start | bytes 2138120 | tf_op jit(solution)/shard_map/ppermute | solution.py:18
  38.9 16.7 %copy-start.1 = (bf16[1,3584,1024]{2,1,0:T(8,128)(2,1)S(1)}, bf16[1,3584,1024]{2,1,0:T(8,128)(2,1)}, u32[]{:S(2)}) copy-start(bf16[1,3584,1024]{2,1,0:T(8,128)(2,1)} %param.13) | copy-start | bytes 22020100
  49.8 3.2 %collective-permute-start.11 = (bf16[96,3584]{1,0:T(8,128)(2,1)S(1)}, bf16[96,3584]{1,0:T(8,128)(2,1)S(1)}, u32[]{:S(2)}, u32[]{:S(2)}) collective-permute-start(bf16[96,3584]{1,0:T(8,128)(2,1)S(1)} %get-tuple-element.150), channel_id=1, source_target_pairs={{0,1},{1,0},{2,3},{3,2},{4,5},{5,4},{6,7},{7,6},{8,9},{9,8},{10,11... | collective-permute-start | bytes 2064392 | tf_op jit(solution)/shard_map/ppermute | solution.py:18
  50.3 19.7 %collective-permute-start.7 = (bf16[96,3712]{1,0:T(8,128)(2,1)S(1)}, bf16[96,3712]{1,0:T(8,128)(2,1)S(1)}, u32[]{:S(2)}, u32[]{:S(2)}) collective-permute-start(bf16[96,3712]{1,0:T(8,128)(2,1)S(1)} %collective-permute-done.3.refs_0_), channel_id=1, source_target_pairs={{0,4},{1,5},{2,6},{3,7},{4,8},{5,9},{6,10},{7,11},{8,12},{9,13},{1... | collective-permute-start | bytes 2138120 | tf_op jit(solution)/shard_map/ppermute | solution.py:18
  51.9 18.1 %collective-permute-start.8 = (bf16[96,3712]{1,0:T(8,128)(2,1)S(1)}, bf16[96,3712]{1,0:T(8,128)(2,1)S(1)}, u32[]{:S(2)}, u32[]{:S(2)}) collective-permute-start(bf16[96,3712]{1,0:T(8,128)(2,1)S(1)} %collective-permute-done.3.refs_0_), channel_id=1, source_target_pairs={{0,2},{1,3},{2,0},{3,1},{4,6},{5,7},{6,4},{7,5},{8,10},{9,11},{10,... | collective-permute-start | bytes 2138120 | tf_op jit(solution)/shard_map/ppermute | solution.py:18
  52.5 17.5 %collective-permute-start.9 = (bf16[96,3712]{1,0:T(8,128)(2,1)S(1)}, bf16[96,3712]{1,0:T(8,128)(2,1)S(1)}, u32[]{:S(2)}, u32[]{:S(2)}) collective-permute-start(bf16[96,3712]{1,0:T(8,128)(2,1)S(1)} %collective-permute-done.3.refs_0_), channel_id=1, source_target_pairs={{0,1},{1,0},{2,3},{3,2},{4,5},{5,4},{6,7},{7,6},{8,9},{9,8},{10,11... | collective-permute-start | bytes 2138120 | tf_op jit(solution)/shard_map/ppermute | solution.py:18
  52.5 3.2 %collective-permute-start.10 = (bf16[96,3712]{1,0:T(8,128)(2,1)S(1)}, bf16[96,3712]{1,0:T(8,128)(2,1)S(1)}, u32[]{:S(2)}, u32[]{:S(2)}) collective-permute-start(bf16[96,3712]{1,0:T(8,128)(2,1)S(1)} %collective-permute-done.4.refs_1_), channel_id=1, source_target_pairs={{0,1},{1,0},{2,3},{3,2},{4,5},{5,4},{6,7},{7,6},{8,9},{9,8},{10,11... | collective-permute-start | bytes 2138120 | tf_op jit(solution)/shard_map/ppermute | solution.py:18
  53.0 20.8 %slice-start = ((s8[7340032]{0:T(1024)(128)(4,1)}), s8[4194304]{0:T(1024)(128)(4,1)S(1)}, s32[]{:S(2)}) async-start(s8[7340032]{0:T(1024)(128)(4,1)} %bitcast.33), calls=%async_computation | async-start | bytes 8388608
  53.0 20.8 %slice-start.2 = ((s8[7340032]{0:T(1024)(128)(4,1)}), s8[4194304]{0:T(1024)(128)(4,1)S(1)}, s32[]{:S(2)}) async-start(s8[7340032]{0:T(1024)(128)(4,1)} %bitcast.43), calls=%async_computation.2 | async-start | bytes 8388608
  53.9 19.9 %slice-start.1 = ((s8[7340032]{0:T(1024)(128)(4,1)}), s8[3145728]{0:T(1024)(128)(4,1)S(1)}, s32[]{:S(2)}) async-start(s8[7340032]{0:T(1024)(128)(4,1)} %bitcast.33), calls=%async_computation.1 | async-start | bytes 6291456
  53.9 19.9 %slice-start.3 = ((s8[7340032]{0:T(1024)(128)(4,1)}), s8[3145728]{0:T(1024)(128)(4,1)S(1)}, s32[]{:S(2)}) async-start(s8[7340032]{0:T(1024)(128)(4,1)} %bitcast.43), calls=%async_computation.3 | async-start | bytes 6291456
  70.0 2.7 %collective-permute-start.16 = (bf16[96,3584]{1,0:T(8,128)(2,1)S(1)}, bf16[96,3584]{1,0:T(8,128)(2,1)S(1)}, u32[]{:S(2)}, u32[]{:S(2)}) collective-permute-start(bf16[96,3584]{1,0:T(8,128)(2,1)S(1)} %get-tuple-element.160), channel_id=1, source_target_pairs={{0,1},{1,0},{2,3},{3,2},{4,5},{5,4},{6,7},{7,6},{8,9},{9,8},{10,11... | collective-permute-start | bytes 2064392 | tf_op jit(solution)/shard_map/ppermute | solution.py:18
  70.0 3.8 %collective-permute-start.15 = (bf16[96,3712]{1,0:T(8,128)(2,1)S(1)}, bf16[96,3712]{1,0:T(8,128)(2,1)S(1)}, u32[]{:S(2)}, u32[]{:S(2)}) collective-permute-start(bf16[96,3712]{1,0:T(8,128)(2,1)S(1)} %collective-permute-done.8.refs_1_), channel_id=1, source_target_pairs={{0,1},{1,0},{2,3},{3,2},{4,5},{5,4},{6,7},{7,6},{8,9},{9,8},{10,11... | collective-permute-start | bytes 2138120 | tf_op jit(solution)/shard_map/ppermute | solution.py:18
  70.5 15.2 %collective-permute-start.14 = (bf16[96,3712]{1,0:T(8,128)(2,1)S(1)}, bf16[96,3712]{1,0:T(8,128)(2,1)S(1)}, u32[]{:S(2)}, u32[]{:S(2)}) collective-permute-start(bf16[96,3712]{1,0:T(8,128)(2,1)S(1)} %collective-permute-done.7.refs_0_), channel_id=1, source_target_pairs={{0,1},{1,0},{2,3},{3,2},{4,5},{5,4},{6,7},{7,6},{8,9},{9,8},{10,11... | collective-permute-start | bytes 2138120 | tf_op jit(solution)/shard_map/ppermute | solution.py:18
  70.7 15.1 %collective-permute-start.13 = (bf16[64,3712]{1,0:T(8,128)(2,1)S(1)}, bf16[64,3712]{1,0:T(8,128)(2,1)S(1)}, u32[]{:S(2)}, u32[]{:S(2)}) collective-permute-start(bf16[64,3712]{1,0:T(8,128)(2,1)S(1)} %slice.131), channel_id=1, source_target_pairs={{0,4},{1,5},{2,6},{3,7},{4,8},{5,9},{6,10},{7,11},{8,12},{9,13},{1... | collective-permute-start | bytes 1425416 | tf_op jit(solution)/shard_map/ppermute | solution.py:18
  71.2 11.3 %collective-permute-start.12 = (bf16[32,3712]{1,0:T(8,128)(2,1)S(1)}, bf16[32,3712]{1,0:T(8,128)(2,1)S(1)}, u32[]{:S(2)}, u32[]{:S(2)}) collective-permute-start(bf16[32,3712]{1,0:T(8,128)(2,1)S(1)} %slice.130), channel_id=1, source_target_pairs={{0,2},{1,3},{2,0},{3,1},{4,6},{5,7},{6,4},{7,5},{8,10},{9,11},{10,... | collective-permute-start | bytes 712712 | tf_op jit(solution)/shard_map/ppermute | solution.py:18
  72.9 13.6 %collective-permute-start.17 = (bf16[48,3584]{1,0:T(8,128)(2,1)S(1)}, bf16[48,3584]{1,0:T(8,128)(2,1)S(1)}, u32[]{:S(2)}, u32[]{:S(2)}) collective-permute-start(bf16[48,3584]{1,0:T(8,128)(2,1)S(1)} %get-tuple-element.276), channel_id=1, source_target_pairs={{0,2},{1,3},{2,0},{3,1},{4,6},{5,7},{6,4},{7,5},{8,10},{9,11},{10,... | collective-permute-start | bytes 1032200 | tf_op jit(solution)/shard_map/ppermute | solution.py:18
  86.5 13.4 %collective-permute-start.21 = (bf16[48,3584]{1,0:T(8,128)(2,1)S(1)}, bf16[48,3584]{1,0:T(8,128)(2,1)S(1)}, u32[]{:S(2)}, u32[]{:S(2)}) collective-permute-start(bf16[48,3584]{1,0:T(8,128)(2,1)S(1)} %add_convert_fusion.17), channel_id=1, source_target_pairs={{0,4},{1,5},{2,6},{3,7},{4,8},{5,9},{6,10},{7,11},{8,12},{9,13},{1... | collective-permute-start | bytes 1032200 | tf_op jit(solution)/shard_map/ppermute | solution.py:18
  88.0 2.1 collective-permute-start.19
  88.1 3.1 %collective-permute-start.18 = (bf16[96,3712]{1,0:T(8,128)(2,1)S(1)}, bf16[96,3712]{1,0:T(8,128)(2,1)S(1)}, u32[]{:S(2)}, u32[]{:S(2)}) collective-permute-start(bf16[96,3712]{1,0:T(8,128)(2,1)S(1)} %constant_dynamic-update-slice_fusion.refs_1_), channel_id=1, source_target_pairs={{0,1},{1,0},{2,3},{3,2},{4,5},{5,4},{6,7},{7,6},{8,9},{9,8},{10,11... | collective-permute-start | bytes 2138120 | tf_op jit(solution)/shard_map/ppermute | solution.py:18
  90.4 24.2 %copy-start.9 = (bf16[48,3584]{1,0:T(8,128)(2,1)S(1)}, bf16[48,3584]{1,0:T(8,128)(2,1)}, u32[]{:S(2)}) copy-start(bf16[48,3584]{1,0:T(8,128)(2,1)} %get-tuple-element.185) | copy-start | bytes 1032196
  90.4 10.2 %collective-permute-start.20 = (bf16[48,3584]{1,0:T(8,128)(2,1)S(1)}, bf16[48,3584]{1,0:T(8,128)(2,1)S(1)}, u32[]{:S(2)}, u32[]{:S(2)}) collective-permute-start(bf16[48,3584]{1,0:T(8,128)(2,1)S(1)} %get-tuple-element.274), channel_id=1, source_target_pairs={{0,2},{1,3},{2,0},{3,1},{4,6},{5,7},{6,4},{7,5},{8,10},{9,11},{10,... | collective-permute-start | bytes 1032200 | tf_op jit(solution)/shard_map/ppermute | solution.py:18
  100.5 2.1 collective-permute-start.22
  100.7 12.3 %collective-permute-start.24 = (bf16[48,3584]{1,0:T(8,128)(2,1)S(1)}, bf16[48,3584]{1,0:T(8,128)(2,1)S(1)}, u32[]{:S(2)}, u32[]{:S(2)}) collective-permute-start(bf16[48,3584]{1,0:T(8,128)(2,1)S(1)} %add_convert_fusion.14), channel_id=1, source_target_pairs={{0,4},{1,5},{2,6},{3,7},{4,8},{5,9},{6,10},{7,11},{8,12},{9,13},{1... | collective-permute-start | bytes 1032200 | tf_op jit(solution)/shard_map/ppermute | solution.py:18
  102.8 10.2 %collective-permute-start.23 = (bf16[48,3584]{1,0:T(8,128)(2,1)S(1)}, bf16[48,3584]{1,0:T(8,128)(2,1)S(1)}, u32[]{:S(2)}, u32[]{:S(2)}) collective-permute-start(bf16[48,3584]{1,0:T(8,128)(2,1)S(1)} %get-tuple-element.272), channel_id=1, source_target_pairs={{0,2},{1,3},{2,0},{3,1},{4,6},{5,7},{6,4},{7,5},{8,10},{9,11},{10,... | collective-permute-start | bytes 1032200 | tf_op jit(solution)/shard_map/ppermute | solution.py:18
  113.1 11.5 %collective-permute-start.26 = (bf16[48,3584]{1,0:T(8,128)(2,1)S(1)}, bf16[48,3584]{1,0:T(8,128)(2,1)S(1)}, u32[]{:S(2)}, u32[]{:S(2)}) collective-permute-start(bf16[48,3584]{1,0:T(8,128)(2,1)S(1)} %add_convert_fusion.13), channel_id=1, source_target_pairs={{0,4},{1,5},{2,6},{3,7},{4,8},{5,9},{6,10},{7,11},{8,12},{9,13},{1... | collective-permute-start | bytes 1032200 | tf_op jit(solution)/shard_map/ppermute | solution.py:18
  114.6 10.1 %collective-permute-start.25 = (bf16[48,3584]{1,0:T(8,128)(2,1)S(1)}, bf16[48,3584]{1,0:T(8,128)(2,1)S(1)}, u32[]{:S(2)}, u32[]{:S(2)}) collective-permute-start(bf16[48,3584]{1,0:T(8,128)(2,1)S(1)} %copy-done.9), channel_id=1, source_target_pairs={{0,2},{1,3},{2,0},{3,1},{4,6},{5,7},{6,4},{7,5},{8,10},{9,11},{10,... | collective-permute-start | bytes 1032200 | tf_op jit(solution)/shard_map/ppermute | solution.py:18
  124.8 10.6 %collective-permute-start.27 = (bf16[48,3584]{1,0:T(8,128)(2,1)S(1)}, bf16[48,3584]{1,0:T(8,128)(2,1)S(1)}, u32[]{:S(2)}, u32[]{:S(2)}) collective-permute-start(bf16[48,3584]{1,0:T(8,128)(2,1)S(1)} %add_convert_fusion.12.refs_0_), channel_id=1, source_target_pairs={{0,4},{1,5},{2,6},{3,7},{4,8},{5,9},{6,10},{7,11},{8,12},{9,13},{1... | collective-permute-start | bytes 1032200 | tf_op jit(solution)/shard_map/ppermute | solution.py:18
  125.6 9.8 %collective-permute-start.28 = (bf16[48,3584]{1,0:T(8,128)(2,1)S(1)}, bf16[48,3584]{1,0:T(8,128)(2,1)S(1)}, u32[]{:S(2)}, u32[]{:S(2)}) collective-permute-start(bf16[48,3584]{1,0:T(8,128)(2,1)S(1)} %add_convert_fusion.12.refs_0_), channel_id=1, source_target_pairs={{0,2},{1,3},{2,0},{3,1},{4,6},{5,7},{6,4},{7,5},{8,10},{9,11},{10,... | collective-permute-start | bytes 1032200 | tf_op jit(solution)/shard_map/ppermute | solution.py:18
  127.0 8.5 %collective-permute-start.29 = (bf16[48,3584]{1,0:T(8,128)(2,1)S(1)}, bf16[48,3584]{1,0:T(8,128)(2,1)S(1)}, u32[]{:S(2)}, u32[]{:S(2)}) collective-permute-start(bf16[48,3584]{1,0:T(8,128)(2,1)S(1)} %add_convert_fusion.12.refs_0_), channel_id=1, source_target_pairs={{0,1},{1,0},{2,3},{3,2},{4,5},{5,4},{6,7},{7,6},{8,9},{9,8},{10,11... | collective-permute-start | bytes 1032200 | tf_op jit(solution)/shard_map/ppermute | solution.py:18
  135.5 1.7 collective-permute-start.33
  135.5 12.3 %collective-permute-start.30 = (bf16[48,3584]{1,0:T(8,128)(2,1)S(1)}, bf16[48,3584]{1,0:T(8,128)(2,1)S(1)}, u32[]{:S(2)}, u32[]{:S(2)}) collective-permute-start(bf16[48,3584]{1,0:T(8,128)(2,1)S(1)} %collective-permute-done.27.refs_0_), channel_id=1, source_target_pairs={{0,4},{1,5},{2,6},{3,7},{4,8},{5,9},{6,10},{7,11},{8,12},{9,13},{1... | collective-permute-start | bytes 1032200 | tf_op jit(solution)/shard_map/ppermute | solution.py:18
  135.5 12.2 %collective-permute-start.31 = (bf16[48,3584]{1,0:T(8,128)(2,1)S(1)}, bf16[48,3584]{1,0:T(8,128)(2,1)S(1)}, u32[]{:S(2)}, u32[]{:S(2)}) collective-permute-start(bf16[48,3584]{1,0:T(8,128)(2,1)S(1)} %collective-permute-done.27.refs_0_), channel_id=1, source_target_pairs={{0,2},{1,3},{2,0},{3,1},{4,6},{5,7},{6,4},{7,5},{8,10},{9,11},{10,... | collective-permute-start | bytes 1032200 | tf_op jit(solution)/shard_map/ppermute | solution.py:18
  136.3 11.5 %collective-permute-start.32 = (bf16[48,3584]{1,0:T(8,128)(2,1)S(1)}, bf16[48,3584]{1,0:T(8,128)(2,1)S(1)}, u32[]{:S(2)}, u32[]{:S(2)}) collective-permute-start(bf16[48,3584]{1,0:T(8,128)(2,1)S(1)} %collective-permute-done.27.refs_0_), channel_id=1, source_target_pairs={{0,1},{1,0},{2,3},{3,2},{4,5},{5,4},{6,7},{7,6},{8,9},{9,8},{10,11... | collective-permute-start | bytes 1032200 | tf_op jit(solution)/shard_map/ppermute | solution.py:18
  147.7 1.7 collective-permute-start.37
  147.7 10.5 %collective-permute-start.38 = (bf16[96,3584]{1,0:T(8,128)(2,1)S(1)}, bf16[96,3584]{1,0:T(8,128)(2,1)S(1)}, u32[]{:S(2)}, u32[]{:S(2)}) collective-permute-start(bf16[96,3584]{1,0:T(8,128)(2,1)S(1)} %get-tuple-element.211), channel_id=1, source_target_pairs={{0,1},{1,0},{2,3},{3,2},{4,5},{5,4},{6,7},{7,6},{8,9},{9,8},{10,11... | collective-permute-start | bytes 2064392 | tf_op jit(solution)/shard_map/ppermute | solution.py:18
  148.2 11.8 %collective-permute-start.34 = (bf16[48,3584]{1,0:T(8,128)(2,1)S(1)}, bf16[48,3584]{1,0:T(8,128)(2,1)S(1)}, u32[]{:S(2)}, u32[]{:S(2)}) collective-permute-start(bf16[48,3584]{1,0:T(8,128)(2,1)S(1)} %collective-permute-done.30.refs_0_), channel_id=1, source_target_pairs={{0,4},{1,5},{2,6},{3,7},{4,8},{5,9},{6,10},{7,11},{8,12},{9,13},{1... | collective-permute-start | bytes 1032200 | tf_op jit(solution)/shard_map/ppermute | solution.py:18
  148.3 11.8 %collective-permute-start.35 = (bf16[48,3584]{1,0:T(8,128)(2,1)S(1)}, bf16[48,3584]{1,0:T(8,128)(2,1)S(1)}, u32[]{:S(2)}, u32[]{:S(2)}) collective-permute-start(bf16[48,3584]{1,0:T(8,128)(2,1)S(1)} %collective-permute-done.30.refs_0_), channel_id=1, source_target_pairs={{0,2},{1,3},{2,0},{3,1},{4,6},{5,7},{6,4},{7,5},{8,10},{9,11},{10,... | collective-permute-start | bytes 1032200 | tf_op jit(solution)/shard_map/ppermute | solution.py:18
  148.9 11.2 %collective-permute-start.36 = (bf16[48,3584]{1,0:T(8,128)(2,1)S(1)}, bf16[48,3584]{1,0:T(8,128)(2,1)S(1)}, u32[]{:S(2)}, u32[]{:S(2)}) collective-permute-start(bf16[48,3584]{1,0:T(8,128)(2,1)S(1)} %collective-permute-done.30.refs_0_), channel_id=1, source_target_pairs={{0,1},{1,0},{2,3},{3,2},{4,5},{5,4},{6,7},{7,6},{8,9},{9,8},{10,11... | collective-permute-start | bytes 1032200 | tf_op jit(solution)/shard_map/ppermute | solution.py:18
  160.1 1.7 collective-permute-start.41
  160.1 10.5 %collective-permute-start.42 = (bf16[96,3584]{1,0:T(8,128)(2,1)S(1)}, bf16[96,3584]{1,0:T(8,128)(2,1)S(1)}, u32[]{:S(2)}, u32[]{:S(2)}) collective-permute-start(bf16[96,3584]{1,0:T(8,128)(2,1)S(1)} %get-tuple-element.223), channel_id=1, source_target_pairs={{0,1},{1,0},{2,3},{3,2},{4,5},{5,4},{6,7},{7,6},{8,9},{9,8},{10,11... | collective-permute-start | bytes 2064392 | tf_op jit(solution)/shard_map/ppermute | solution.py:18
  160.6 10.2 %collective-permute-start.39 = (bf16[48,3584]{1,0:T(8,128)(2,1)S(1)}, bf16[48,3584]{1,0:T(8,128)(2,1)S(1)}, u32[]{:S(2)}, u32[]{:S(2)}) collective-permute-start(bf16[48,3584]{1,0:T(8,128)(2,1)S(1)} %collective-permute-done.34.refs_0_), channel_id=1, source_target_pairs={{0,2},{1,3},{2,0},{3,1},{4,6},{5,7},{6,4},{7,5},{8,10},{9,11},{10,... | collective-permute-start | bytes 1032200 | tf_op jit(solution)/shard_map/ppermute | solution.py:18
  161.3 9.5 %collective-permute-start.40 = (bf16[48,3584]{1,0:T(8,128)(2,1)S(1)}, bf16[48,3584]{1,0:T(8,128)(2,1)S(1)}, u32[]{:S(2)}, u32[]{:S(2)}) collective-permute-start(bf16[48,3584]{1,0:T(8,128)(2,1)S(1)} %collective-permute-done.34.refs_0_), channel_id=1, source_target_pairs={{0,1},{1,0},{2,3},{3,2},{4,5},{5,4},{6,7},{7,6},{8,9},{9,8},{10,11... | collective-permute-start | bytes 1032200 | tf_op jit(solution)/shard_map/ppermute | solution.py:18
  170.8 1.7 collective-permute-start.43
  171.0 10.4 %collective-permute-start.44 = (bf16[96,3584]{1,0:T(8,128)(2,1)S(1)}, bf16[96,3584]{1,0:T(8,128)(2,1)S(1)}, u32[]{:S(2)}, u32[]{:S(2)}) collective-permute-start(bf16[96,3584]{1,0:T(8,128)(2,1)S(1)} %get-tuple-element.236), channel_id=1, source_target_pairs={{0,1},{1,0},{2,3},{3,2},{4,5},{5,4},{6,7},{7,6},{8,9},{9,8},{10,11... | collective-permute-start | bytes 2064392 | tf_op jit(solution)/shard_map/ppermute | solution.py:18
  171.4 10.2 %collective-permute-start.45 = (bf16[48,3584]{1,0:T(8,128)(2,1)S(1)}, bf16[48,3584]{1,0:T(8,128)(2,1)S(1)}, u32[]{:S(2)}, u32[]{:S(2)}) collective-permute-start(bf16[48,3584]{1,0:T(8,128)(2,1)S(1)} %get-tuple-element.237), channel_id=1, source_target_pairs={{0,2},{1,3},{2,0},{3,1},{4,6},{5,7},{6,4},{7,5},{8,10},{9,11},{10,... | collective-permute-start | bytes 1032200 | tf_op jit(solution)/shard_map/ppermute | solution.py:18
  181.7 2.0 collective-permute-start.49
  181.9 2.2 %collective-permute-start.46 = (bf16[96,3584]{1,0:T(8,128)(2,1)S(1)}, bf16[96,3584]{1,0:T(8,128)(2,1)S(1)}, u32[]{:S(2)}, u32[]{:S(2)}) collective-permute-start(bf16[96,3584]{1,0:T(8,128)(2,1)S(1)} %get-tuple-element.241), channel_id=1, source_target_pairs={{0,1},{1,0},{2,3},{3,2},{4,5},{5,4},{6,7},{7,6},{8,9},{9,8},{10,11... | collective-permute-start | bytes 2064392 | tf_op jit(solution)/shard_map/ppermute | solution.py:18
  182.4 12.0 %collective-permute-start.48 = (bf16[48,3584]{1,0:T(8,128)(2,1)S(1)}, bf16[48,3584]{1,0:T(8,128)(2,1)S(1)}, u32[]{:S(2)}, u32[]{:S(2)}) collective-permute-start(bf16[48,3584]{1,0:T(8,128)(2,1)S(1)} %add_convert_fusion.3), channel_id=1, source_target_pairs={{0,4},{1,5},{2,6},{3,7},{4,8},{5,9},{6,10},{7,11},{8,12},{9,13},{1... | collective-permute-start | bytes 1032200 | tf_op jit(solution)/shard_map/ppermute | solution.py:18
  182.4 11.9 %collective-permute-start.47 = (bf16[48,3584]{1,0:T(8,128)(2,1)S(1)}, bf16[48,3584]{1,0:T(8,128)(2,1)S(1)}, u32[]{:S(2)}, u32[]{:S(2)}) collective-permute-start(bf16[48,3584]{1,0:T(8,128)(2,1)S(1)} %get-tuple-element.242), channel_id=1, source_target_pairs={{0,2},{1,3},{2,0},{3,1},{4,6},{5,7},{6,4},{7,5},{8,10},{9,11},{10,... | collective-permute-start | bytes 1032200 | tf_op jit(solution)/shard_map/ppermute | solution.py:18
  194.4 11.1 %collective-permute-start.51 = (bf16[48,3584]{1,0:T(8,128)(2,1)S(1)}, bf16[48,3584]{1,0:T(8,128)(2,1)S(1)}, u32[]{:S(2)}, u32[]{:S(2)}) collective-permute-start(bf16[48,3584]{1,0:T(8,128)(2,1)S(1)} %add_convert_fusion.2), channel_id=1, source_target_pairs={{0,4},{1,5},{2,6},{3,7},{4,8},{5,9},{6,10},{7,11},{8,12},{9,13},{1... | collective-permute-start | bytes 1032200 | tf_op jit(solution)/shard_map/ppermute | solution.py:18
  194.5 11.1 %collective-permute-start.50 = (bf16[48,3584]{1,0:T(8,128)(2,1)S(1)}, bf16[48,3584]{1,0:T(8,128)(2,1)S(1)}, u32[]{:S(2)}, u32[]{:S(2)}) collective-permute-start(bf16[48,3584]{1,0:T(8,128)(2,1)S(1)} %get-tuple-element.248), channel_id=1, source_target_pairs={{0,2},{1,3},{2,0},{3,1},{4,6},{5,7},{6,4},{7,5},{8,10},{9,11},{10,... | collective-permute-start | bytes 1032200 | tf_op jit(solution)/shard_map/ppermute | solution.py:18
  195.8 9.4 %collective-permute-start.52 = (f32[4,16,224]{2,1,0:T(8,128)S(1)}, f32[4,16,224]{2,1,0:T(8,128)S(1)}, u32[]{:S(2)}, u32[]{:S(2)}) collective-permute-start(f32[4,16,224]{2,1,0:T(8,128)S(1)} %slice_bitcast_fusion), channel_id=1, source_target_pairs={{0,2},{1,3},{2,0},{3,1},{4,6},{5,7},{6,4},{7,5},{8,10},{9,11},{10,... | collective-permute-start | bytes 172040 | tf_op jit(solution)/shard_map/ppermute | solution.py:18
  205.7 12.2 %collective-permute-start.54 = (bf16[48,3584]{1,0:T(8,128)(2,1)S(1)}, bf16[48,3584]{1,0:T(8,128)(2,1)S(1)}, u32[]{:S(2)}, u32[]{:S(2)}) collective-permute-start(bf16[48,3584]{1,0:T(8,128)(2,1)S(1)} %add_convert_fusion.1), channel_id=1, source_target_pairs={{0,4},{1,5},{2,6},{3,7},{4,8},{5,9},{6,10},{7,11},{8,12},{9,13},{1... | collective-permute-start | bytes 1032200 | tf_op jit(solution)/shard_map/ppermute | solution.py:18
  206.4 11.6 %collective-permute-start.53 = (bf16[48,3584]{1,0:T(8,128)(2,1)S(1)}, bf16[48,3584]{1,0:T(8,128)(2,1)S(1)}, u32[]{:S(2)}, u32[]{:S(2)}) collective-permute-start(bf16[48,3584]{1,0:T(8,128)(2,1)S(1)} %get-tuple-element.256), channel_id=1, source_target_pairs={{0,2},{1,3},{2,0},{3,1},{4,6},{5,7},{6,4},{7,5},{8,10},{9,11},{10,... | collective-permute-start | bytes 1032200 | tf_op jit(solution)/shard_map/ppermute | solution.py:18
  207.4 6.4 %collective-permute-start.55 = (f32[16,224]{1,0:T(8,128)S(1)}, f32[16,224]{1,0:T(8,128)S(1)}, u32[]{:S(2)}, u32[]{:S(2)}) collective-permute-start(f32[16,224]{1,0:T(8,128)S(1)} %get-tuple-element.280), channel_id=1, source_target_pairs={{0,12},{1,13},{2,14},{3,15},{4,0},{5,1},{6,2},{7,3},{8,4},{9,5},{1... | collective-permute-start | bytes 43016 | tf_op jit(solution)/shard_map/ppermute | solution.py:18
  210.9 6.4 %collective-permute-start.56 = (f32[16,224]{1,0:T(8,128)S(1)}, f32[16,224]{1,0:T(8,128)S(1)}, u32[]{:S(2)}, u32[]{:S(2)}) collective-permute-start(f32[16,224]{1,0:T(8,128)S(1)} %get-tuple-element.282), channel_id=1, source_target_pairs={{0,8},{1,9},{2,10},{3,11},{4,12},{5,13},{6,14},{7,15},{8,0},{9,1},... | collective-permute-start | bytes 43016 | tf_op jit(solution)/shard_map/ppermute | solution.py:18
  210.9 6.4 %collective-permute-start.57 = (f32[16,224]{1,0:T(8,128)S(1)}, f32[16,224]{1,0:T(8,128)S(1)}, u32[]{:S(2)}, u32[]{:S(2)}) collective-permute-start(f32[16,224]{1,0:T(8,128)S(1)} %get-tuple-element.281), channel_id=1, source_target_pairs={{0,4},{1,5},{2,6},{3,7},{4,8},{5,9},{6,10},{7,11},{8,12},{9,13},{1... | collective-permute-start | bytes 43016 | tf_op jit(solution)/shard_map/ppermute | solution.py:18
  (8 other events, 15.1 us)
where the time goes:
time: 219 us
  waiting for transfers between devices  85 us (39%)
  Pallas kernels  73.5 us (34%)
  starting transfers between devices  39.6 us (18%)
  local copies, waits for them, and re-layouts  15.2 us (7%)
  other arithmetic  4.3 us (2%)
    ppermute x58, waiting for transfers between devices, swap(): return lax.ppermute(values, 'expert', perm)  85 us
    ppermute x58, starting transfers between devices, swap(): return lax.ppermute(values, 'expert', perm)  39.6 us
    pallas_call x4, Pallas kernels, up_call(): pl.pallas_call(functools.partial(up_kernel, tile_of(hidden, 512), tile_of...  36 us
    pallas_call x4, Pallas kernels, down_call(): pl.pallas_call(functools.partial(down_kernel, tile_of(hidden, 512), tile_...  35.3 us
    unnamed x29, local copies, waits for them, and re-layouts  15.1 us
  transfers between devices with their start and end apart: 58, of which 24 were waited for; matrix products, arithmetic and copies ran while one was open for 1% of the time, Pallas kernels for 33%

commit v1 on v0

--- a/solution.py
+++ b/solution.py
@@ -249,8 +249,8 @@
             if turn < depth - 1:
                 flight["near"] = swap(near[turn], ring)
                 flight["far"] = swap(near[turn], across)
-            elif split is None:
-                flight["far"] = swap(near[turn], across)
+            elif split == 0:
+                flight["far"] = swap(far[turn - 1], ring)
             else:
                 flight["far_low"] = swap(near[turn][:split], across)
                 flight["far_high"] = swap(far[turn - 1][split:], ring)
@@ -344,10 +344,9 @@
     def side(turn, terms):
         if turn == depth + 1:
             term = arrange_call(held["sum"], mine, count)
-            held["sum"] = term[:2] + swap(term[2:], pair)
+            term = term[:2] + swap(term[2:], pair)
+            held["sum"] = term[0] + swap(term[1], across)
         elif turn == depth + 2:
-            held["sum"] = held["sum"][0] + swap(held["sum"][1], across)
-        elif turn == depth + 3:
             term = held["sum"]
             total = term[0]
             for s in range(1, depth):
@@ -362,7 +361,7 @@
         held["sum"] = values
 
     turns = {s + 1: s for s in range(depth)}
-    curvature_rows, _, sketch = phase(combined, None, 0, down, turns, (side, settle), ring, across, pair, depth)
+    curvature_rows, _, sketch = phase(combined, 0, 1, down, turns, (side, settle), ring, across, pair, depth)
     return (curvature_rows, sketch)
 
 

time: 219 us -> 214 us (0.977)
  local copies, waits for them, and re-layouts: 15.2 us -> 12.5 us
    unnamed x29 -> x25, local copies, waits for them, and re-layouts: 15.1 us -> 12.4 us
  transfers between devices with their start and end apart: 58 -> 58, of which waited for: 24 -> 27; matrix products, arithmetic and copies ran while one was open for 1% -> 1% of each run, Pallas kernels for 33% -> 33%
where the time goes in v1:
time: 214 us; the launch traced here: 213 us
  waiting for transfers between devices  84.3 us (39%)
  Pallas kernels  73.6 us (34%)
  starting transfers between devices  37.5 us (18%)
  local copies, waits for them, and re-layouts  12.5 us (6%)
  other arithmetic  4.32 us (2%)
    ppermute x58, waiting for transfers between devices, swap(): return lax.ppermute(values, 'expert', perm)  84.3 us
    ppermute x58, starting transfers between devices, swap(): return lax.ppermute(values, 'expert', perm)  37.5 us
    pallas_call x4, Pallas kernels, up_call(): pl.pallas_call(functools.partial(up_kernel, tile_of(hidden, 512), tile_of...  36 us
    pallas_call x4, Pallas kernels, down_call(): pl.pallas_call(functools.partial(down_kernel, tile_of(hidden, 512), tile_...  35.3 us
    unnamed x25, local copies, waits for them, and re-layouts  12.4 us
  transfers between devices with their start and end apart: 58, of which 27 were waited for; matrix products, arithmetic and copies ran while one was open for 1% of the time, Pallas kernels for 33%

profile of v1, /device:TPU:0, one launch (start us, length us, event | category | flops | bytes accessed | tf_op | source)
XLA Modules:
  0.0 213.2 jit_solution(5633407144050937106)
XLA Ops:
  0.6 2.1 shard_map.95.refs_0_
  2.7 3.1 %collective-permute-start = (bf16[96,3712]{1,0:T(8,128)(2,1)}, bf16[96,3712]{1,0:T(8,128)(2,1)S(1)}, u32[]{:S(2)}, u32[]{:S(2)}) collective-permute-start(bf16[96,3712]{1,0:T(8,128)(2,1)} %shard_map.95.refs_0_), channel_id=1, source_target_pairs={{0,4},{1,5},{2,6},{3,7},{4,8},{5,9},{6,10},{7,11},{8,12},{9,13},{1... | collective-permute-start | bytes 2138120 | tf_op jit(solution)/shard_map/ppermute | solution.py:18
  5.8 1.5 collective-permute-start.1
  7.3 16.7 %collective-permute-done.refs_0_ = bf16[96,3712]{1,0:T(8,128)(2,1)S(1)} collective-permute-done((bf16[96,3712]{1,0:T(8,128)(2,1)}, bf16[96,3712]{1,0:T(8,128)(2,1)S(1)}, u32[]{:S(2)}, u32[]{:S(2)}) %collective-permute-start) | collective-permute-done | bytes 712736 | tf_op jit(solution)/shard_map/ppermute | solution.py:18
  24.0 0.9 copy-done.5
  24.9 1.1 collective-permute-start.3
  26.0 1.5 collective-permute-start.4
  27.5 3.1 %copy-done = bf16[1,3584,1024]{2,1,0:T(8,128)(2,1)S(1)} copy-done((bf16[1,3584,1024]{2,1,0:T(8,128)(2,1)S(1)}, bf16[1,3584,1024]{2,1,0:T(8,128)(2,1)}, u32[]{:S(2)}) %copy-start) | copy-done | bytes 7340056
  30.6 3.1 %copy-done.2 = bf16[1,3584,1024]{2,1,0:T(8,128)(2,1)S(1)} copy-done((bf16[1,3584,1024]{2,1,0:T(8,128)(2,1)S(1)}, bf16[1,3584,1024]{2,1,0:T(8,128)(2,1)}, u32[]{:S(2)}) %copy-start.2) | copy-done | bytes 7340056
  33.7 3.1 %copy-done.3 = bf16[1,1024,3584]{2,1,0:T(8,128)(2,1)S(1)} copy-done((bf16[1,1024,3584]{2,1,0:T(8,128)(2,1)S(1)}, bf16[1,1024,3584]{2,1,0:T(8,128)(2,1)}, u32[]{:S(2)}) %copy-start.3) | copy-done | bytes 7340056
  36.8 1.1 copy-done.4
  37.9 1.1 copy-done.6
  39.0 10.0 %shard_map.96 = (bf16[96,3584]{1,0:T(8,128)(2,1)S(1)}, bf16[96,3584]{1,0:T(8,128)(2,1)S(1)}, f32[192,1024]{1,0:T(8,128)S(1)}, f32[192,1024]{1,0:T(8,128)S(1)}, bf16[128,192]{1,0:T(8,128)(2,1)S(1)}) custom-call(bf16[96,3712]{1,0:T(8,128)(2,1)S(1)} %copy-done.4, bf16[96,3712]{1,0:T(8,128)(2,1)} %collective-permute-done.1.refs_1_, ...), custom_call_target="tpu_custom_call" | custom-call | flops 7046430720 | bytes 1048576 | tf_op jit(solution)/shard_map/pallas_call | solution.py:182
  49.0 0.6 collective-permute-start.11
  49.6 1.6 collective-permute-start.7
  51.1 0.6 collective-permute-start.8
  52.2 0.9 add_convert_fusion.22
  53.1 1.8 collective-permute-done.10.refs_3_
  54.9 8.7 %shard_map.97 = (bf16[96,3584]{1,0:T(8,128)(2,1)S(1)}, bf16[96,3584]{1,0:T(8,128)(2,1)S(1)}, f32[192,1024]{1,0:T(8,128)S(1)}, f32[192,1024]{1,0:T(8,128)S(1)}, bf16[128,192]{1,0:T(8,128)(2,1)S(1)}) custom-call(bf16[96,3712]{1,0:T(8,128)(2,1)S(1)} %collective-permute-done.refs_0_, bf16[96,3712]{1,0:T(8,128)(2,1)S(1)} %collective-permute-done.4.refs_1_, ...), custom_call_target="tpu_custom_call" | custom-call | flops 7046430720 | bytes 1048576 | tf_op jit(solution)/shard_map/pallas_call | solution.py:182
  63.6 5.7 %collective-permute-done.7.refs_0_ = bf16[96,3712]{1,0:T(8,128)(2,1)S(1)} collective-permute-done((bf16[96,3712]{1,0:T(8,128)(2,1)S(1)}, bf16[96,3712]{1,0:T(8,128)(2,1)S(1)}, u32[]{:S(2)}, u32[]{:S(2)}) %collective-permute-start.7) | collective-permute-done | bytes 712736 | tf_op jit(solution)/shard_map/ppermute | solution.py:18
  70.4 1.5 collective-permute-start.12
  72.1 0.9 collective-permute-start.17
  73.0 8.7 %shard_map.98 = (bf16[96,3584]{1,0:T(8,128)(2,1)S(1)}, bf16[96,3584]{1,0:T(8,128)(2,1)S(1)}, f32[192,1024]{1,0:T(8,128)S(1)}, f32[192,1024]{1,0:T(8,128)S(1)}, bf16[128,192]{1,0:T(8,128)(2,1)S(1)}) custom-call(bf16[96,3712]{1,0:T(8,128)(2,1)S(1)} %collective-permute-done.3.refs_0_, bf16[96,3712]{1,0:T(8,128)(2,1)S(1)} %collective-permute-done.8.refs_1_, ...), custom_call_target="tpu_custom_call" | custom-call | flops 7046430720 | bytes 1048576 | tf_op jit(solution)/shard_map/pallas_call | solution.py:182
  81.8 3.3 %collective-permute-done.13 = bf16[64,3712]{1,0:T(8,128)(2,1)S(1)} collective-permute-done((bf16[64,3712]{1,0:T(8,128)(2,1)S(1)}, bf16[64,3712]{1,0:T(8,128)(2,1)S(1)}, u32[]{:S(2)}, u32[]{:S(2)}) %collective-permute-start.13) | collective-permute-done | bytes 475168 | tf_op jit(solution)/shard_map/ppermute | solution.py:18
  85.1 0.6 collective-permute-done.17
  85.8 1.6 collective-permute-start.21
  88.0 1.5 collective-permute-done.19
  89.7 0.6 collective-permute-start.20
  90.5 8.7 %shard_map.99 = (bf16[96,3584]{1,0:T(8,128)(2,1)S(1)}, bf16[96,3584]{1,0:T(8,128)(2,1)S(1)}, f32[192,1024]{1,0:T(8,128)S(1)}, f32[192,1024]{1,0:T(8,128)S(1)}, bf16[128,192]{1,0:T(8,128)(2,1)S(1)}) custom-call(bf16[96,3712]{1,0:T(8,128)(2,1)S(1)} %collective-permute-done.7.refs_0_, bf16[96,3712]{1,0:T(8,128)(2,1)S(1)} %constant_dynamic-update-slice_fusion.refs_1_, ...), custom_call_target="tpu_custom_call" | custom-call | flops 7046430720 | bytes 1048576 | tf_op jit(solution)/shard_map/pallas_call | solution.py:182
  99.2 0.6 collective-permute-done.20
  100.0 1.2 collective-permute-start.24
  101.2 0.8 collective-permute-done.22
  102.1 0.8 collective-permute-start.23
  102.9 9.4 %collective-permute-done.24 = bf16[48,3584]{1,0:T(8,128)(2,1)S(1)} collective-permute-done((bf16[48,3584]{1,0:T(8,128)(2,1)S(1)}, bf16[48,3584]{1,0:T(8,128)(2,1)S(1)}, u32[]{:S(2)}, u32[]{:S(2)}) %collective-permute-start.24) | collective-permute-done | bytes 344096 | tf_op jit(solution)/shard_map/ppermute | solution.py:18
  112.4 1.4 collective-permute-start.26
  113.8 1.3 collective-permute-start.25
  115.2 8.8 %collective-permute-done.26 = bf16[48,3584]{1,0:T(8,128)(2,1)S(1)} collective-permute-done((bf16[48,3584]{1,0:T(8,128)(2,1)S(1)}, bf16[48,3584]{1,0:T(8,128)(2,1)S(1)}, u32[]{:S(2)}, u32[]{:S(2)}) %collective-permute-start.26) | collective-permute-done | bytes 344096 | tf_op jit(solution)/shard_map/ppermute | solution.py:18
  124.1 0.8 collective-permute-start.27
  124.9 1.3 collective-permute-start.28
  126.2 8.5 %collective-permute-done.27.refs_0_ = bf16[48,3584]{1,0:T(8,128)(2,1)S(1)} collective-permute-done((bf16[48,3584]{1,0:T(8,128)(2,1)S(1)}, bf16[48,3584]{1,0:T(8,128)(2,1)S(1)}, u32[]{:S(2)}, u32[]{:S(2)}) %collective-permute-start.27) | collective-permute-done | bytes 344096 | tf_op jit(solution)/shard_map/ppermute | solution.py:18
  134.8 0.8 collective-permute-start.31
  135.7 0.7 collective-permute-done.33.refs_3_
  136.4 8.8 %shard_map.100 = (bf16[96,3584]{1,0:T(8,128)(2,1)S(1)}, bf16[96,3584]{1,0:T(8,128)(2,1)S(1)}, f32[16,3584]{1,0:T(8,128)S(1)}) custom-call(bf16[48,3584]{1,0:T(8,128)(2,1)S(1)} %add_convert_fusion.12.refs_0_, bf16[48,3584]{1,0:T(8,128)(2,1)S(1)} %collective-permute-done.28.refs_1_, bf16[48,3584]{1,0:T(8,128)(2,1)S(1)} %collective-permute-done.29.refs_2_, ...), custom_call_target="tpu_custom_call" | custom-call | flops 4227858432 | bytes 1048576 | tf_op jit(solution)/shard_map/pallas_call | solution.py:205
  145.3 1.8 collective-permute-done.30.refs_0_
  147.6 0.7 collective-permute-start.35
  148.7 8.8 %shard_map.101 = (bf16[96,3584]{1,0:T(8,128)(2,1)S(1)}, bf16[96,3584]{1,0:T(8,128)(2,1)S(1)}, f32[16,3584]{1,0:T(8,128)S(1)}) custom-call(bf16[48,3584]{1,0:T(8,128)(2,1)S(1)} %collective-permute-done.27.refs_0_, bf16[48,3584]{1,0:T(8,128)(2,1)S(1)} %collective-permute-done.31.refs_1_, bf16[48,3584]{1,0:T(8,128)(2,1)S(1)} %collective-permute-done.32.refs_2_, ...), custom_call_target="tpu_custom_call" | custom-call | flops 4227858432 | bytes 1048576 | tf_op jit(solution)/shard_map/pallas_call | solution.py:205
  157.7 1.7 collective-permute-done.34.refs_0_
  160.0 1.6 collective-permute-done.42
  161.7 0.7 collective-permute-start.43
  162.5 8.8 %shard_map.102 = (bf16[96,3584]{1,0:T(8,128)(2,1)S(1)}, bf16[96,3584]{1,0:T(8,128)(2,1)S(1)}, f32[16,3584]{1,0:T(8,128)S(1)}) custom-call(bf16[48,3584]{1,0:T(8,128)(2,1)S(1)} %collective-permute-done.30.refs_0_, bf16[48,3584]{1,0:T(8,128)(2,1)S(1)} %collective-permute-done.35.refs_1_, bf16[48,3584]{1,0:T(8,128)(2,1)S(1)} %collective-permute-done.36.refs_2_, ...), custom_call_target="tpu_custom_call" | custom-call | flops 4227858432 | bytes 1048576 | tf_op jit(solution)/shard_map/pallas_call | solution.py:205
  172.6 1.4 collective-permute-done.45
  174.2 0.9 collective-permute-start.46
  175.1 8.8 %shard_map.103 = (bf16[96,3584]{1,0:T(8,128)(2,1)S(1)}, bf16[96,3584]{1,0:T(8,128)(2,1)S(1)}, f32[16,3584]{1,0:T(8,128)S(1)}) custom-call(bf16[48,3584]{1,0:T(8,128)(2,1)S(1)} %collective-permute-done.34.refs_0_, bf16[48,3584]{1,0:T(8,128)(2,1)S(1)} %collective-permute-done.39.refs_1_, bf16[48,3584]{1,0:T(8,128)(2,1)S(1)} %collective-permute-done.40.refs_2_, ...), custom_call_target="tpu_custom_call" | custom-call | flops 4227858432 | bytes 1048576 | tf_op jit(solution)/shard_map/pallas_call | solution.py:205
  185.9 1.0 collective-permute-done.48
  187.1 0.9 collective-permute-start.49
  188.0 1.2 collective-permute-start.52
  189.2 9.7 %collective-permute-done.52 = f32[4,16,224]{2,1,0:T(8,128)S(1)} collective-permute-done((f32[4,16,224]{2,1,0:T(8,128)S(1)}, f32[4,16,224]{2,1,0:T(8,128)S(1)}, u32[]{:S(2)}, u32[]{:S(2)}) %collective-permute-start.52) | collective-permute-done | bytes 57376 | tf_op jit(solution)/shard_map/ppermute | solution.py:18
  199.2 1.3 collective-permute-start.53
  200.5 3.2 %collective-permute-start.55 = (f32[16,224]{1,0:T(8,128)S(1)}, f32[16,224]{1,0:T(8,128)S(1)}, u32[]{:S(2)}, u32[]{:S(2)}) collective-permute-start(f32[16,224]{1,0:T(8,128)S(1)} %get-tuple-element.268), channel_id=1, source_target_pairs={{0,12},{1,13},{2,14},{3,15},{4,0},{5,1},{6,2},{7,3},{8,4},{9,5},{1... | collective-permute-start | bytes 43016 | tf_op jit(solution)/shard_map/ppermute | solution.py:18
  203.7 1.4 collective-permute-start.57
  205.1 4.1 %collective-permute-done.55 = f32[16,224]{1,0:T(8,128)S(1)} collective-permute-done((f32[16,224]{1,0:T(8,128)S(1)}, f32[16,224]{1,0:T(8,128)S(1)}, u32[]{:S(2)}, u32[]{:S(2)}) %collective-permute-start.55) | collective-permute-done | bytes 14368 | tf_op jit(solution)/shard_map/ppermute | solution.py:18
  209.3 2.5 %collective-permute-done.56 = f32[16,224]{1,0:T(8,128)S(1)} collective-permute-done((f32[16,224]{1,0:T(8,128)S(1)}, f32[16,224]{1,0:T(8,128)S(1)}, u32[]{:S(2)}, u32[]{:S(2)}) %collective-permute-start.56) | collective-permute-done | bytes 14368 | tf_op jit(solution)/shard_map/ppermute | solution.py:18
  211.7 0.6 fusion.2
  212.4 0.9 add_convert_fusion
  (115 shorter events, 9.5 us)
Async XLA Ops:
  2.7 21.3 %collective-permute-start = (bf16[96,3712]{1,0:T(8,128)(2,1)}, bf16[96,3712]{1,0:T(8,128)(2,1)S(1)}, u32[]{:S(2)}, u32[]{:S(2)}) collective-permute-start(bf16[96,3712]{1,0:T(8,128)(2,1)} %shard_map.95.refs_0_), channel_id=1, source_target_pairs={{0,4},{1,5},{2,6},{3,7},{4,8},{5,9},{6,10},{7,11},{8,12},{9,13},{1... | collective-permute-start | bytes 2138120 | tf_op jit(solution)/shard_map/ppermute | solution.py:18
  5.8 18.2 %collective-permute-start.1 = (bf16[96,3712]{1,0:T(8,128)(2,1)}, bf16[96,3712]{1,0:T(8,128)(2,1)}, u32[]{:S(2)}, u32[]{:S(2)}) collective-permute-start(bf16[96,3712]{1,0:T(8,128)(2,1)} %shard_map.95.refs_0_), channel_id=1, source_target_pairs={{0,2},{1,3},{2,0},{3,1},{4,6},{5,7},{6,4},{7,5},{8,10},{9,11},{10,... | collective-permute-start | bytes 2138120 | tf_op jit(solution)/shard_map/ppermute | solution.py:18
  7.3 16.7 %collective-permute-start.2 = (bf16[96,3712]{1,0:T(8,128)(2,1)}, bf16[96,3712]{1,0:T(8,128)(2,1)S(1)}, u32[]{:S(2)}, u32[]{:S(2)}) collective-permute-start(bf16[96,3712]{1,0:T(8,128)(2,1)} %shard_map.95.refs_0_), channel_id=1, source_target_pairs={{0,1},{1,0},{2,3},{3,2},{4,5},{5,4},{6,7},{7,6},{8,9},{9,8},{10,11... | collective-permute-start | bytes 2138120 | tf_op jit(solution)/shard_map/ppermute | solution.py:18
  24.9 2.6 %collective-permute-start.6 = (bf16[96,3712]{1,0:T(8,128)(2,1)}, bf16[96,3712]{1,0:T(8,128)(2,1)}, u32[]{:S(2)}, u32[]{:S(2)}) collective-permute-start(bf16[96,3712]{1,0:T(8,128)(2,1)} %collective-permute-done.1.refs_1_), channel_id=1, source_target_pairs={{0,1},{1,0},{2,3},{3,2},{4,5},{5,4},{6,7},{7,6},{8,9},{9,8},{10,11... | collective-permute-start | bytes 2138120 | tf_op jit(solution)/shard_map/ppermute | solution.py:18
  24.9 24.1 %collective-permute-start.3 = (bf16[96,3712]{1,0:T(8,128)(2,1)S(1)}, bf16[96,3712]{1,0:T(8,128)(2,1)S(1)}, u32[]{:S(2)}, u32[]{:S(2)}) collective-permute-start(bf16[96,3712]{1,0:T(8,128)(2,1)S(1)} %collective-permute-done.refs_0_), channel_id=1, source_target_pairs={{0,4},{1,5},{2,6},{3,7},{4,8},{5,9},{6,10},{7,11},{8,12},{9,13},{1... | collective-permute-start | bytes 2138120 | tf_op jit(solution)/shard_map/ppermute | solution.py:18
  26.0 23.0 %collective-permute-start.4 = (bf16[96,3712]{1,0:T(8,128)(2,1)S(1)}, bf16[96,3712]{1,0:T(8,128)(2,1)S(1)}, u32[]{:S(2)}, u32[]{:S(2)}) collective-permute-start(bf16[96,3712]{1,0:T(8,128)(2,1)S(1)} %collective-permute-done.refs_0_), channel_id=1, source_target_pairs={{0,2},{1,3},{2,0},{3,1},{4,6},{5,7},{6,4},{7,5},{8,10},{9,11},{10,... | collective-permute-start | bytes 2138120 | tf_op jit(solution)/shard_map/ppermute | solution.py:18
  27.5 21.5 %collective-permute-start.5 = (bf16[96,3712]{1,0:T(8,128)(2,1)S(1)}, bf16[96,3712]{1,0:T(8,128)(2,1)S(1)}, u32[]{:S(2)}, u32[]{:S(2)}) collective-permute-start(bf16[96,3712]{1,0:T(8,128)(2,1)S(1)} %collective-permute-done.refs_0_), channel_id=1, source_target_pairs={{0,1},{1,0},{2,3},{3,2},{4,5},{5,4},{6,7},{7,6},{8,9},{9,8},{10,11... | collective-permute-start | bytes 2138120 | tf_op jit(solution)/shard_map/ppermute | solution.py:18
  39.0 15.9 %copy-start.1 = (bf16[1,3584,1024]{2,1,0:T(8,128)(2,1)S(1)}, bf16[1,3584,1024]{2,1,0:T(8,128)(2,1)}, u32[]{:S(2)}) copy-start(bf16[1,3584,1024]{2,1,0:T(8,128)(2,1)} %param.13) | copy-start | bytes 22020100
  49.0 3.2 %collective-permute-start.11 = (bf16[96,3584]{1,0:T(8,128)(2,1)S(1)}, bf16[96,3584]{1,0:T(8,128)(2,1)S(1)}, u32[]{:S(2)}, u32[]{:S(2)}) collective-permute-start(bf16[96,3584]{1,0:T(8,128)(2,1)S(1)} %get-tuple-element.144), channel_id=1, source_target_pairs={{0,1},{1,0},{2,3},{3,2},{4,5},{5,4},{6,7},{7,6},{8,9},{9,8},{10,11... | collective-permute-start | bytes 2064392 | tf_op jit(solution)/shard_map/ppermute | solution.py:18
  49.6 19.7 %collective-permute-start.7 = (bf16[96,3712]{1,0:T(8,128)(2,1)S(1)}, bf16[96,3712]{1,0:T(8,128)(2,1)S(1)}, u32[]{:S(2)}, u32[]{:S(2)}) collective-permute-start(bf16[96,3712]{1,0:T(8,128)(2,1)S(1)} %collective-permute-done.3.refs_0_), channel_id=1, source_target_pairs={{0,4},{1,5},{2,6},{3,7},{4,8},{5,9},{6,10},{7,11},{8,12},{9,13},{1... | collective-permute-start | bytes 2138120 | tf_op jit(solution)/shard_map/ppermute | solution.py:18
  51.1 18.2 %collective-permute-start.8 = (bf16[96,3712]{1,0:T(8,128)(2,1)S(1)}, bf16[96,3712]{1,0:T(8,128)(2,1)S(1)}, u32[]{:S(2)}, u32[]{:S(2)}) collective-permute-start(bf16[96,3712]{1,0:T(8,128)(2,1)S(1)} %collective-permute-done.3.refs_0_), channel_id=1, source_target_pairs={{0,2},{1,3},{2,0},{3,1},{4,6},{5,7},{6,4},{7,5},{8,10},{9,11},{10,... | collective-permute-start | bytes 2138120 | tf_op jit(solution)/shard_map/ppermute | solution.py:18
  51.7 17.6 %collective-permute-start.9 = (bf16[96,3712]{1,0:T(8,128)(2,1)S(1)}, bf16[96,3712]{1,0:T(8,128)(2,1)S(1)}, u32[]{:S(2)}, u32[]{:S(2)}) collective-permute-start(bf16[96,3712]{1,0:T(8,128)(2,1)S(1)} %collective-permute-done.3.refs_0_), channel_id=1, source_target_pairs={{0,1},{1,0},{2,3},{3,2},{4,5},{5,4},{6,7},{7,6},{8,9},{9,8},{10,11... | collective-permute-start | bytes 2138120 | tf_op jit(solution)/shard_map/ppermute | solution.py:18
  51.7 3.2 %collective-permute-start.10 = (bf16[96,3712]{1,0:T(8,128)(2,1)S(1)}, bf16[96,3712]{1,0:T(8,128)(2,1)S(1)}, u32[]{:S(2)}, u32[]{:S(2)}) collective-permute-start(bf16[96,3712]{1,0:T(8,128)(2,1)S(1)} %collective-permute-done.4.refs_1_), channel_id=1, source_target_pairs={{0,1},{1,0},{2,3},{3,2},{4,5},{5,4},{6,7},{7,6},{8,9},{9,8},{10,11... | collective-permute-start | bytes 2138120 | tf_op jit(solution)/shard_map/ppermute | solution.py:18
  52.2 20.8 %slice-start = ((s8[7340032]{0:T(1024)(128)(4,1)}), s8[4194304]{0:T(1024)(128)(4,1)S(1)}, s32[]{:S(2)}) async-start(s8[7340032]{0:T(1024)(128)(4,1)} %bitcast.35), calls=%async_computation | async-start | bytes 8388608
  52.2 20.8 %slice-start.2 = ((s8[7340032]{0:T(1024)(128)(4,1)}), s8[4194304]{0:T(1024)(128)(4,1)S(1)}, s32[]{:S(2)}) async-start(s8[7340032]{0:T(1024)(128)(4,1)} %bitcast.45), calls=%async_computation.2 | async-start | bytes 8388608
  53.1 19.9 %slice-start.1 = ((s8[7340032]{0:T(1024)(128)(4,1)}), s8[3145728]{0:T(1024)(128)(4,1)S(1)}, s32[]{:S(2)}) async-start(s8[7340032]{0:T(1024)(128)(4,1)} %bitcast.35), calls=%async_computation.1 | async-start | bytes 6291456
  53.1 19.9 %slice-start.3 = ((s8[7340032]{0:T(1024)(128)(4,1)}), s8[3145728]{0:T(1024)(128)(4,1)S(1)}, s32[]{:S(2)}) async-start(s8[7340032]{0:T(1024)(128)(4,1)} %bitcast.45), calls=%async_computation.3 | async-start | bytes 6291456
  69.3 2.6 %collective-permute-start.16 = (bf16[96,3584]{1,0:T(8,128)(2,1)S(1)}, bf16[96,3584]{1,0:T(8,128)(2,1)S(1)}, u32[]{:S(2)}, u32[]{:S(2)}) collective-permute-start(bf16[96,3584]{1,0:T(8,128)(2,1)S(1)} %get-tuple-element.154), channel_id=1, source_target_pairs={{0,1},{1,0},{2,3},{3,2},{4,5},{5,4},{6,7},{7,6},{8,9},{9,8},{10,11... | collective-permute-start | bytes 2064392 | tf_op jit(solution)/shard_map/ppermute | solution.py:18
  69.3 3.7 %collective-permute-start.15 = (bf16[96,3712]{1,0:T(8,128)(2,1)S(1)}, bf16[96,3712]{1,0:T(8,128)(2,1)S(1)}, u32[]{:S(2)}, u32[]{:S(2)}) collective-permute-start(bf16[96,3712]{1,0:T(8,128)(2,1)S(1)} %collective-permute-done.8.refs_1_), channel_id=1, source_target_pairs={{0,1},{1,0},{2,3},{3,2},{4,5},{5,4},{6,7},{7,6},{8,9},{9,8},{10,11... | collective-permute-start | bytes 2138120 | tf_op jit(solution)/shard_map/ppermute | solution.py:18
  69.8 15.2 %collective-permute-start.14 = (bf16[96,3712]{1,0:T(8,128)(2,1)S(1)}, bf16[96,3712]{1,0:T(8,128)(2,1)S(1)}, u32[]{:S(2)}, u32[]{:S(2)}) collective-permute-start(bf16[96,3712]{1,0:T(8,128)(2,1)S(1)} %collective-permute-done.7.refs_0_), channel_id=1, source_target_pairs={{0,1},{1,0},{2,3},{3,2},{4,5},{5,4},{6,7},{7,6},{8,9},{9,8},{10,11... | collective-permute-start | bytes 2138120 | tf_op jit(solution)/shard_map/ppermute | solution.py:18
  70.0 15.1 %collective-permute-start.13 = (bf16[64,3712]{1,0:T(8,128)(2,1)S(1)}, bf16[64,3712]{1,0:T(8,128)(2,1)S(1)}, u32[]{:S(2)}, u32[]{:S(2)}) collective-permute-start(bf16[64,3712]{1,0:T(8,128)(2,1)S(1)} %slice.131), channel_id=1, source_target_pairs={{0,4},{1,5},{2,6},{3,7},{4,8},{5,9},{6,10},{7,11},{8,12},{9,13},{1... | collective-permute-start | bytes 1425416 | tf_op jit(solution)/shard_map/ppermute | solution.py:18
  70.4 11.3 %collective-permute-start.12 = (bf16[32,3712]{1,0:T(8,128)(2,1)S(1)}, bf16[32,3712]{1,0:T(8,128)(2,1)S(1)}, u32[]{:S(2)}, u32[]{:S(2)}) collective-permute-start(bf16[32,3712]{1,0:T(8,128)(2,1)S(1)} %slice.130), channel_id=1, source_target_pairs={{0,2},{1,3},{2,0},{3,1},{4,6},{5,7},{6,4},{7,5},{8,10},{9,11},{10,... | collective-permute-start | bytes 712712 | tf_op jit(solution)/shard_map/ppermute | solution.py:18
  72.1 13.6 %collective-permute-start.17 = (bf16[48,3584]{1,0:T(8,128)(2,1)S(1)}, bf16[48,3584]{1,0:T(8,128)(2,1)S(1)}, u32[]{:S(2)}, u32[]{:S(2)}) collective-permute-start(bf16[48,3584]{1,0:T(8,128)(2,1)S(1)} %get-tuple-element.264), channel_id=1, source_target_pairs={{0,2},{1,3},{2,0},{3,1},{4,6},{5,7},{6,4},{7,5},{8,10},{9,11},{10,... | collective-permute-start | bytes 1032200 | tf_op jit(solution)/shard_map/ppermute | solution.py:18
  85.8 13.4 %collective-permute-start.21 = (bf16[48,3584]{1,0:T(8,128)(2,1)S(1)}, bf16[48,3584]{1,0:T(8,128)(2,1)S(1)}, u32[]{:S(2)}, u32[]{:S(2)}) collective-permute-start(bf16[48,3584]{1,0:T(8,128)(2,1)S(1)} %add_convert_fusion.17), channel_id=1, source_target_pairs={{0,4},{1,5},{2,6},{3,7},{4,8},{5,9},{6,10},{7,11},{8,12},{9,13},{1... | collective-permute-start | bytes 1032200 | tf_op jit(solution)/shard_map/ppermute | solution.py:18
  87.3 2.1 %collective-permute-start.19 = (bf16[96,3584]{1,0:T(8,128)(2,1)S(1)}, bf16[96,3584]{1,0:T(8,128)(2,1)S(1)}, u32[]{:S(2)}, u32[]{:S(2)}) collective-permute-start(bf16[96,3584]{1,0:T(8,128)(2,1)S(1)} %get-tuple-element.166), channel_id=1, source_target_pairs={{0,1},{1,0},{2,3},{3,2},{4,5},{5,4},{6,7},{7,6},{8,9},{9,8},{10,11... | collective-permute-start | bytes 2064392 | tf_op jit(solution)/shard_map/ppermute | solution.py:18
  87.4 3.1 %collective-permute-start.18 = (bf16[96,3712]{1,0:T(8,128)(2,1)S(1)}, bf16[96,3712]{1,0:T(8,128)(2,1)S(1)}, u32[]{:S(2)}, u32[]{:S(2)}) collective-permute-start(bf16[96,3712]{1,0:T(8,128)(2,1)S(1)} %constant_dynamic-update-slice_fusion.refs_1_), channel_id=1, source_target_pairs={{0,1},{1,0},{2,3},{3,2},{4,5},{5,4},{6,7},{7,6},{8,9},{9,8},{10,11... | collective-permute-start | bytes 2138120 | tf_op jit(solution)/shard_map/ppermute | solution.py:18
  89.6 24.2 %copy-start.7 = (bf16[48,3584]{1,0:T(8,128)(2,1)S(1)}, bf16[48,3584]{1,0:T(8,128)(2,1)}, u32[]{:S(2)}) copy-start(bf16[48,3584]{1,0:T(8,128)(2,1)} %get-tuple-element.179) | copy-start | bytes 1032196
  89.7 10.2 %collective-permute-start.20 = (bf16[48,3584]{1,0:T(8,128)(2,1)S(1)}, bf16[48,3584]{1,0:T(8,128)(2,1)S(1)}, u32[]{:S(2)}, u32[]{:S(2)}) collective-permute-start(bf16[48,3584]{1,0:T(8,128)(2,1)S(1)} %get-tuple-element.262), channel_id=1, source_target_pairs={{0,2},{1,3},{2,0},{3,1},{4,6},{5,7},{6,4},{7,5},{8,10},{9,11},{10,... | collective-permute-start | bytes 1032200 | tf_op jit(solution)/shard_map/ppermute | solution.py:18
  99.8 2.1 %collective-permute-start.22 = (bf16[96,3584]{1,0:T(8,128)(2,1)S(1)}, bf16[96,3584]{1,0:T(8,128)(2,1)S(1)}, u32[]{:S(2)}, u32[]{:S(2)}) collective-permute-start(bf16[96,3584]{1,0:T(8,128)(2,1)S(1)} %get-tuple-element.172), channel_id=1, source_target_pairs={{0,1},{1,0},{2,3},{3,2},{4,5},{5,4},{6,7},{7,6},{8,9},{9,8},{10,11... | collective-permute-start | bytes 2064392 | tf_op jit(solution)/shard_map/ppermute | solution.py:18
  100.0 12.3 %collective-permute-start.24 = (bf16[48,3584]{1,0:T(8,128)(2,1)S(1)}, bf16[48,3584]{1,0:T(8,128)(2,1)S(1)}, u32[]{:S(2)}, u32[]{:S(2)}) collective-permute-start(bf16[48,3584]{1,0:T(8,128)(2,1)S(1)} %add_convert_fusion.14), channel_id=1, source_target_pairs={{0,4},{1,5},{2,6},{3,7},{4,8},{5,9},{6,10},{7,11},{8,12},{9,13},{1... | collective-permute-start | bytes 1032200 | tf_op jit(solution)/shard_map/ppermute | solution.py:18
  102.1 10.2 %collective-permute-start.23 = (bf16[48,3584]{1,0:T(8,128)(2,1)S(1)}, bf16[48,3584]{1,0:T(8,128)(2,1)S(1)}, u32[]{:S(2)}, u32[]{:S(2)}) collective-permute-start(bf16[48,3584]{1,0:T(8,128)(2,1)S(1)} %get-tuple-element.260), channel_id=1, source_target_pairs={{0,2},{1,3},{2,0},{3,1},{4,6},{5,7},{6,4},{7,5},{8,10},{9,11},{10,... | collective-permute-start | bytes 1032200 | tf_op jit(solution)/shard_map/ppermute | solution.py:18
  112.4 11.5 %collective-permute-start.26 = (bf16[48,3584]{1,0:T(8,128)(2,1)S(1)}, bf16[48,3584]{1,0:T(8,128)(2,1)S(1)}, u32[]{:S(2)}, u32[]{:S(2)}) collective-permute-start(bf16[48,3584]{1,0:T(8,128)(2,1)S(1)} %add_convert_fusion.13), channel_id=1, source_target_pairs={{0,4},{1,5},{2,6},{3,7},{4,8},{5,9},{6,10},{7,11},{8,12},{9,13},{1... | collective-permute-start | bytes 1032200 | tf_op jit(solution)/shard_map/ppermute | solution.py:18
  113.8 10.1 %collective-permute-start.25 = (bf16[48,3584]{1,0:T(8,128)(2,1)S(1)}, bf16[48,3584]{1,0:T(8,128)(2,1)S(1)}, u32[]{:S(2)}, u32[]{:S(2)}) collective-permute-start(bf16[48,3584]{1,0:T(8,128)(2,1)S(1)} %copy-done.7), channel_id=1, source_target_pairs={{0,2},{1,3},{2,0},{3,1},{4,6},{5,7},{6,4},{7,5},{8,10},{9,11},{10,... | collective-permute-start | bytes 1032200 | tf_op jit(solution)/shard_map/ppermute | solution.py:18
  124.1 10.6 %collective-permute-start.27 = (bf16[48,3584]{1,0:T(8,128)(2,1)S(1)}, bf16[48,3584]{1,0:T(8,128)(2,1)S(1)}, u32[]{:S(2)}, u32[]{:S(2)}) collective-permute-start(bf16[48,3584]{1,0:T(8,128)(2,1)S(1)} %add_convert_fusion.12.refs_0_), channel_id=1, source_target_pairs={{0,4},{1,5},{2,6},{3,7},{4,8},{5,9},{6,10},{7,11},{8,12},{9,13},{1... | collective-permute-start | bytes 1032200 | tf_op jit(solution)/shard_map/ppermute | solution.py:18
  124.9 9.9 %collective-permute-start.28 = (bf16[48,3584]{1,0:T(8,128)(2,1)S(1)}, bf16[48,3584]{1,0:T(8,128)(2,1)S(1)}, u32[]{:S(2)}, u32[]{:S(2)}) collective-permute-start(bf16[48,3584]{1,0:T(8,128)(2,1)S(1)} %add_convert_fusion.12.refs_0_), channel_id=1, source_target_pairs={{0,2},{1,3},{2,0},{3,1},{4,6},{5,7},{6,4},{7,5},{8,10},{9,11},{10,... | collective-permute-start | bytes 1032200 | tf_op jit(solution)/shard_map/ppermute | solution.py:18
  126.2 8.5 %collective-permute-start.29 = (bf16[48,3584]{1,0:T(8,128)(2,1)S(1)}, bf16[48,3584]{1,0:T(8,128)(2,1)S(1)}, u32[]{:S(2)}, u32[]{:S(2)}) collective-permute-start(bf16[48,3584]{1,0:T(8,128)(2,1)S(1)} %add_convert_fusion.12.refs_0_), channel_id=1, source_target_pairs={{0,1},{1,0},{2,3},{3,2},{4,5},{5,4},{6,7},{7,6},{8,9},{9,8},{10,11... | collective-permute-start | bytes 1032200 | tf_op jit(solution)/shard_map/ppermute | solution.py:18
  134.8 1.7 collective-permute-start.33
  134.8 12.3 %collective-permute-start.30 = (bf16[48,3584]{1,0:T(8,128)(2,1)S(1)}, bf16[48,3584]{1,0:T(8,128)(2,1)S(1)}, u32[]{:S(2)}, u32[]{:S(2)}) collective-permute-start(bf16[48,3584]{1,0:T(8,128)(2,1)S(1)} %collective-permute-done.27.refs_0_), channel_id=1, source_target_pairs={{0,4},{1,5},{2,6},{3,7},{4,8},{5,9},{6,10},{7,11},{8,12},{9,13},{1... | collective-permute-start | bytes 1032200 | tf_op jit(solution)/shard_map/ppermute | solution.py:18
  134.8 12.2 %collective-permute-start.31 = (bf16[48,3584]{1,0:T(8,128)(2,1)S(1)}, bf16[48,3584]{1,0:T(8,128)(2,1)S(1)}, u32[]{:S(2)}, u32[]{:S(2)}) collective-permute-start(bf16[48,3584]{1,0:T(8,128)(2,1)S(1)} %collective-permute-done.27.refs_0_), channel_id=1, source_target_pairs={{0,2},{1,3},{2,0},{3,1},{4,6},{5,7},{6,4},{7,5},{8,10},{9,11},{10,... | collective-permute-start | bytes 1032200 | tf_op jit(solution)/shard_map/ppermute | solution.py:18
  135.6 11.5 %collective-permute-start.32 = (bf16[48,3584]{1,0:T(8,128)(2,1)S(1)}, bf16[48,3584]{1,0:T(8,128)(2,1)S(1)}, u32[]{:S(2)}, u32[]{:S(2)}) collective-permute-start(bf16[48,3584]{1,0:T(8,128)(2,1)S(1)} %collective-permute-done.27.refs_0_), channel_id=1, source_target_pairs={{0,1},{1,0},{2,3},{3,2},{4,5},{5,4},{6,7},{7,6},{8,9},{9,8},{10,11... | collective-permute-start | bytes 1032200 | tf_op jit(solution)/shard_map/ppermute | solution.py:18
  147.0 1.7 collective-permute-start.37
  147.1 10.5 %collective-permute-start.38 = (bf16[96,3584]{1,0:T(8,128)(2,1)S(1)}, bf16[96,3584]{1,0:T(8,128)(2,1)S(1)}, u32[]{:S(2)}, u32[]{:S(2)}) collective-permute-start(bf16[96,3584]{1,0:T(8,128)(2,1)S(1)} %get-tuple-element.205), channel_id=1, source_target_pairs={{0,1},{1,0},{2,3},{3,2},{4,5},{5,4},{6,7},{7,6},{8,9},{9,8},{10,11... | collective-permute-start | bytes 2064392 | tf_op jit(solution)/shard_map/ppermute | solution.py:18
  147.6 11.8 %collective-permute-start.34 = (bf16[48,3584]{1,0:T(8,128)(2,1)S(1)}, bf16[48,3584]{1,0:T(8,128)(2,1)S(1)}, u32[]{:S(2)}, u32[]{:S(2)}) collective-permute-start(bf16[48,3584]{1,0:T(8,128)(2,1)S(1)} %collective-permute-done.30.refs_0_), channel_id=1, source_target_pairs={{0,4},{1,5},{2,6},{3,7},{4,8},{5,9},{6,10},{7,11},{8,12},{9,13},{1... | collective-permute-start | bytes 1032200 | tf_op jit(solution)/shard_map/ppermute | solution.py:18
  147.6 11.8 %collective-permute-start.35 = (bf16[48,3584]{1,0:T(8,128)(2,1)S(1)}, bf16[48,3584]{1,0:T(8,128)(2,1)S(1)}, u32[]{:S(2)}, u32[]{:S(2)}) collective-permute-start(bf16[48,3584]{1,0:T(8,128)(2,1)S(1)} %collective-permute-done.30.refs_0_), channel_id=1, source_target_pairs={{0,2},{1,3},{2,0},{3,1},{4,6},{5,7},{6,4},{7,5},{8,10},{9,11},{10,... | collective-permute-start | bytes 1032200 | tf_op jit(solution)/shard_map/ppermute | solution.py:18
  148.2 11.2 %collective-permute-start.36 = (bf16[48,3584]{1,0:T(8,128)(2,1)S(1)}, bf16[48,3584]{1,0:T(8,128)(2,1)S(1)}, u32[]{:S(2)}, u32[]{:S(2)}) collective-permute-start(bf16[48,3584]{1,0:T(8,128)(2,1)S(1)} %collective-permute-done.30.refs_0_), channel_id=1, source_target_pairs={{0,1},{1,0},{2,3},{3,2},{4,5},{5,4},{6,7},{7,6},{8,9},{9,8},{10,11... | collective-permute-start | bytes 1032200 | tf_op jit(solution)/shard_map/ppermute | solution.py:18
  159.4 2.1 %collective-permute-start.42 = (bf16[96,3584]{1,0:T(8,128)(2,1)S(1)}, bf16[96,3584]{1,0:T(8,128)(2,1)S(1)}, u32[]{:S(2)}, u32[]{:S(2)}) collective-permute-start(bf16[96,3584]{1,0:T(8,128)(2,1)S(1)} %get-tuple-element.217), channel_id=1, source_target_pairs={{0,1},{1,0},{2,3},{3,2},{4,5},{5,4},{6,7},{7,6},{8,9},{9,8},{10,11... | collective-permute-start | bytes 2064392 | tf_op jit(solution)/shard_map/ppermute | solution.py:18
  159.4 3.0 %collective-permute-start.41 = (bf16[48,3584]{1,0:T(8,128)(2,1)S(1)}, bf16[48,3584]{1,0:T(8,128)(2,1)S(1)}, u32[]{:S(2)}, u32[]{:S(2)}) collective-permute-start(bf16[48,3584]{1,0:T(8,128)(2,1)S(1)} %collective-permute-done.35.refs_1_), channel_id=1, source_target_pairs={{0,1},{1,0},{2,3},{3,2},{4,5},{5,4},{6,7},{7,6},{8,9},{9,8},{10,11... | collective-permute-start | bytes 1032200 | tf_op jit(solution)/shard_map/ppermute | solution.py:18
  159.9 11.8 %collective-permute-start.39 = (bf16[48,3584]{1,0:T(8,128)(2,1)S(1)}, bf16[48,3584]{1,0:T(8,128)(2,1)S(1)}, u32[]{:S(2)}, u32[]{:S(2)}) collective-permute-start(bf16[48,3584]{1,0:T(8,128)(2,1)S(1)} %collective-permute-done.35.refs_1_), channel_id=1, source_target_pairs={{0,4},{1,5},{2,6},{3,7},{4,8},{5,9},{6,10},{7,11},{8,12},{9,13},{1... | collective-permute-start | bytes 1032200 | tf_op jit(solution)/shard_map/ppermute | solution.py:18
  159.9 11.8 %collective-permute-start.40 = (bf16[48,3584]{1,0:T(8,128)(2,1)S(1)}, bf16[48,3584]{1,0:T(8,128)(2,1)S(1)}, u32[]{:S(2)}, u32[]{:S(2)}) collective-permute-start(bf16[48,3584]{1,0:T(8,128)(2,1)S(1)} %collective-permute-done.34.refs_0_), channel_id=1, source_target_pairs={{0,1},{1,0},{2,3},{3,2},{4,5},{5,4},{6,7},{7,6},{8,9},{9,8},{10,11... | collective-permute-start | bytes 1032200 | tf_op jit(solution)/shard_map/ppermute | solution.py:18
  161.7 10.2 %collective-permute-start.43 = (bf16[48,3584]{1,0:T(8,128)(2,1)S(1)}, bf16[48,3584]{1,0:T(8,128)(2,1)S(1)}, u32[]{:S(2)}, u32[]{:S(2)}) collective-permute-start(bf16[48,3584]{1,0:T(8,128)(2,1)S(1)} %get-tuple-element.256), channel_id=1, source_target_pairs={{0,2},{1,3},{2,0},{3,1},{4,6},{5,7},{6,4},{7,5},{8,10},{9,11},{10,... | collective-permute-start | bytes 1032200 | tf_op jit(solution)/shard_map/ppermute | solution.py:18
  171.9 2.1 %collective-permute-start.45 = (bf16[96,3584]{1,0:T(8,128)(2,1)S(1)}, bf16[96,3584]{1,0:T(8,128)(2,1)S(1)}, u32[]{:S(2)}, u32[]{:S(2)}) collective-permute-start(bf16[96,3584]{1,0:T(8,128)(2,1)S(1)} %get-tuple-element.230), channel_id=1, source_target_pairs={{0,1},{1,0},{2,3},{3,2},{4,5},{5,4},{6,7},{7,6},{8,9},{9,8},{10,11... | collective-permute-start | bytes 2064392 | tf_op jit(solution)/shard_map/ppermute | solution.py:18
  172.0 12.3 %collective-permute-start.47 = (bf16[48,3584]{1,0:T(8,128)(2,1)S(1)}, bf16[48,3584]{1,0:T(8,128)(2,1)S(1)}, u32[]{:S(2)}, u32[]{:S(2)}) collective-permute-start(bf16[48,3584]{1,0:T(8,128)(2,1)S(1)} %add_convert_fusion.5), channel_id=1, source_target_pairs={{0,4},{1,5},{2,6},{3,7},{4,8},{5,9},{6,10},{7,11},{8,12},{9,13},{1... | collective-permute-start | bytes 1032200 | tf_op jit(solution)/shard_map/ppermute | solution.py:18
  172.0 3.1 %collective-permute-start.44 = (bf16[48,3584]{1,0:T(8,128)(2,1)S(1)}, bf16[48,3584]{1,0:T(8,128)(2,1)S(1)}, u32[]{:S(2)}, u32[]{:S(2)}) collective-permute-start(bf16[48,3584]{1,0:T(8,128)(2,1)S(1)} %collective-permute-done.39.refs_1_), channel_id=1, source_target_pairs={{0,1},{1,0},{2,3},{3,2},{4,5},{5,4},{6,7},{7,6},{8,9},{9,8},{10,11... | collective-permute-start | bytes 1032200 | tf_op jit(solution)/shard_map/ppermute | solution.py:18
  174.2 10.2 %collective-permute-start.46 = (bf16[48,3584]{1,0:T(8,128)(2,1)S(1)}, bf16[48,3584]{1,0:T(8,128)(2,1)S(1)}, u32[]{:S(2)}, u32[]{:S(2)}) collective-permute-start(bf16[48,3584]{1,0:T(8,128)(2,1)S(1)} %get-tuple-element.254), channel_id=1, source_target_pairs={{0,2},{1,3},{2,0},{3,1},{4,6},{5,7},{6,4},{7,5},{8,10},{9,11},{10,... | collective-permute-start | bytes 1032200 | tf_op jit(solution)/shard_map/ppermute | solution.py:18
  184.5 1.4 collective-permute-start.51
  184.6 2.3 %collective-permute-start.48 = (bf16[96,3584]{1,0:T(8,128)(2,1)S(1)}, bf16[96,3584]{1,0:T(8,128)(2,1)S(1)}, u32[]{:S(2)}, u32[]{:S(2)}) collective-permute-start(bf16[96,3584]{1,0:T(8,128)(2,1)S(1)} %get-tuple-element.236), channel_id=1, source_target_pairs={{0,1},{1,0},{2,3},{3,2},{4,5},{5,4},{6,7},{7,6},{8,9},{9,8},{10,11... | collective-permute-start | bytes 2064392 | tf_op jit(solution)/shard_map/ppermute | solution.py:18
  185.2 13.6 %collective-permute-start.50 = (bf16[48,3584]{1,0:T(8,128)(2,1)S(1)}, bf16[48,3584]{1,0:T(8,128)(2,1)S(1)}, u32[]{:S(2)}, u32[]{:S(2)}) collective-permute-start(bf16[48,3584]{1,0:T(8,128)(2,1)S(1)} %add_convert_fusion.2), channel_id=1, source_target_pairs={{0,4},{1,5},{2,6},{3,7},{4,8},{5,9},{6,10},{7,11},{8,12},{9,13},{1... | collective-permute-start | bytes 1032200 | tf_op jit(solution)/shard_map/ppermute | solution.py:18
  187.1 11.8 %collective-permute-start.49 = (bf16[48,3584]{1,0:T(8,128)(2,1)S(1)}, bf16[48,3584]{1,0:T(8,128)(2,1)S(1)}, u32[]{:S(2)}, u32[]{:S(2)}) collective-permute-start(bf16[48,3584]{1,0:T(8,128)(2,1)S(1)} %get-tuple-element.252), channel_id=1, source_target_pairs={{0,2},{1,3},{2,0},{3,1},{4,6},{5,7},{6,4},{7,5},{8,10},{9,11},{10,... | collective-permute-start | bytes 1032200 | tf_op jit(solution)/shard_map/ppermute | solution.py:18
  188.0 10.8 %collective-permute-start.52 = (f32[4,16,224]{2,1,0:T(8,128)S(1)}, f32[4,16,224]{2,1,0:T(8,128)S(1)}, u32[]{:S(2)}, u32[]{:S(2)}) collective-permute-start(f32[4,16,224]{2,1,0:T(8,128)S(1)} %slice_bitcast_fusion), channel_id=1, source_target_pairs={{0,2},{1,3},{2,0},{3,1},{4,6},{5,7},{6,4},{7,5},{8,10},{9,11},{10,... | collective-permute-start | bytes 172040 | tf_op jit(solution)/shard_map/ppermute | solution.py:18
  199.0 13.4 %collective-permute-start.54 = (bf16[48,3584]{1,0:T(8,128)(2,1)S(1)}, bf16[48,3584]{1,0:T(8,128)(2,1)S(1)}, u32[]{:S(2)}, u32[]{:S(2)}) collective-permute-start(bf16[48,3584]{1,0:T(8,128)(2,1)S(1)} %add_convert_fusion.1), channel_id=1, source_target_pairs={{0,4},{1,5},{2,6},{3,7},{4,8},{5,9},{6,10},{7,11},{8,12},{9,13},{1... | collective-permute-start | bytes 1032200 | tf_op jit(solution)/shard_map/ppermute | solution.py:18
  199.2 13.2 %collective-permute-start.53 = (bf16[48,3584]{1,0:T(8,128)(2,1)S(1)}, bf16[48,3584]{1,0:T(8,128)(2,1)S(1)}, u32[]{:S(2)}, u32[]{:S(2)}) collective-permute-start(bf16[48,3584]{1,0:T(8,128)(2,1)S(1)} %get-tuple-element.244), channel_id=1, source_target_pairs={{0,2},{1,3},{2,0},{3,1},{4,6},{5,7},{6,4},{7,5},{8,10},{9,11},{10,... | collective-permute-start | bytes 1032200 | tf_op jit(solution)/shard_map/ppermute | solution.py:18
  200.5 8.8 %collective-permute-start.55 = (f32[16,224]{1,0:T(8,128)S(1)}, f32[16,224]{1,0:T(8,128)S(1)}, u32[]{:S(2)}, u32[]{:S(2)}) collective-permute-start(f32[16,224]{1,0:T(8,128)S(1)} %get-tuple-element.268), channel_id=1, source_target_pairs={{0,12},{1,13},{2,14},{3,15},{4,0},{5,1},{6,2},{7,3},{8,4},{9,5},{1... | collective-permute-start | bytes 43016 | tf_op jit(solution)/shard_map/ppermute | solution.py:18
  203.7 8.0 %collective-permute-start.56 = (f32[16,224]{1,0:T(8,128)S(1)}, f32[16,224]{1,0:T(8,128)S(1)}, u32[]{:S(2)}, u32[]{:S(2)}) collective-permute-start(f32[16,224]{1,0:T(8,128)S(1)} %get-tuple-element.270), channel_id=1, source_target_pairs={{0,8},{1,9},{2,10},{3,11},{4,12},{5,13},{6,14},{7,15},{8,0},{9,1},... | collective-permute-start | bytes 43016 | tf_op jit(solution)/shard_map/ppermute | solution.py:18
  203.7 8.0 %collective-permute-start.57 = (f32[16,224]{1,0:T(8,128)S(1)}, f32[16,224]{1,0:T(8,128)S(1)}, u32[]{:S(2)}, u32[]{:S(2)}) collective-permute-start(f32[16,224]{1,0:T(8,128)S(1)} %get-tuple-element.269), channel_id=1, source_target_pairs={{0,4},{1,5},{2,6},{3,7},{4,8},{5,9},{6,10},{7,11},{8,12},{9,13},{1... | collective-permute-start | bytes 43016 | tf_op jit(solution)/shard_map/ppermute | solution.py:18
  (6 other events, 12.3 us)
